TPU v7x, 256 devices: a whole 4x4x8 slice. The times are simulated.
256 devices in a mesh: src: 16 (over z, x_hi), rcv: 16 (over x_lo, y, core).
Axes of the slice: x: 4 (x_hi: 2, x_lo: 2; x = x_hi * 2 + x_lo), y: 4, z: 8, core: 2. Of those that a mesh axis runs over, the one named last changes fastest.
Arguments:
- traces: bfloat16 [2, 1024, 3072], P(None, ('src', 'rcv')), may hold values from -6 to 6
- window_valid: int32 [2, 1024], P(None, ('src', 'rcv')), may hold values 0 or 1
- pair_mask: int32 [1024, 1024], P('src', 'rcv'), may hold values from 0 to 1, as said below
Outputs:
- correlations: float32 [1024, 1024, 512], P('src', 'rcv')
Inputs may be any that keep to these rules, and one draw needn't show every extreme that they name: pair_mask[i, j] is 1 exactly where |i - j| lies in a band of offsets drawn for source channel i.
All inputs are finite; a program needn't handle non-finite values. No bound on the sum of `window_valid` on one device may be relied on, other than what follows from the above.
Results may differ from a plain program's by a relative error of at most 0.0064.
Values may be sent and summed in bfloat16 or wider, within the bound.
A program may use at most 128 MiB of HBM per device.

v0:
```python
import math

import jax
import jax.numpy as jnp
from jax import lax
from jax.sharding import PartitionSpec as P

NS = 3072
NF = 1536
LAGS = 512
HALF = 32


EPSILON = 1e-06


def fourier_table(samples, freq_count):
    sample_ids = lax.broadcasted_iota(jnp.int32, (samples, freq_count), 0)
    freq_ids = lax.broadcasted_iota(jnp.int32, (samples, freq_count), 1) + 1
    phases = sample_ids * freq_ids % samples
    angles = phases.astype(jnp.float32) * (2.0 * math.pi / samples)
    return jnp.concatenate([jnp.cos(angles), -jnp.sin(angles)], axis=1).astype(jnp.bfloat16)


def lag_table(samples, freq_count, lag_count):
    freq_ids = lax.broadcasted_iota(jnp.int32, (freq_count, lag_count), 0) + 1
    lag_ids = lax.broadcasted_iota(jnp.int32, (freq_count, lag_count), 1) - lag_count // 2
    phases = jnp.mod(freq_ids * lag_ids, samples)
    angles = phases.astype(jnp.float32) * (2.0 * math.pi / samples)
    return jnp.concatenate([jnp.cos(angles), -jnp.sin(angles)], axis=0).astype(jnp.bfloat16)


def whiten(traces, flags, table, half_width):
    win_count, chan_count, sample_count = traces.shape
    freq_count = table.shape[1] // 2
    spectrum = jnp.dot(
        traces.reshape(win_count * chan_count, sample_count),
        table,
        preferred_element_type=jnp.float32,
    )
    real_part = spectrum[:, :freq_count]
    imag_part = spectrum[:, freq_count:]
    amplitude = jnp.sqrt(real_part * real_part + imag_part * imag_part)
    running = lax.reduce_window(
        amplitude,
        jnp.zeros((), amplitude.dtype),
        lax.add,
        (1, 2 * half_width + 1),
        (1, 1),
        ((0, 0), (half_width, half_width)),
    )
    running = running / (2 * half_width + 1)
    factor = flags.reshape(win_count * chan_count, 1).astype(jnp.float32) / (running + EPSILON)
    whitened = spectrum * jnp.concatenate([factor, factor], axis=1)
    return whitened.astype(jnp.bfloat16).reshape(win_count, chan_count, 2 * freq_count)


def correlate(sources, receivers, source_flags, receiver_flags, mask_block, lags):
    freq_count = sources.shape[2] // 2
    counts = jnp.dot(source_flags.T, receiver_flags, preferred_element_type=jnp.float32)
    src_real = sources[:, :, None, :freq_count].astype(jnp.float32)
    src_imag = sources[:, :, None, freq_count:].astype(jnp.float32)
    rcv_real = receivers[:, None, :, :freq_count].astype(jnp.float32)
    rcv_imag = receivers[:, None, :, freq_count:].astype(jnp.float32)
    cross_real = jnp.sum(src_real * rcv_real + src_imag * rcv_imag, axis=0)
    cross_imag = jnp.sum(src_imag * rcv_real - src_real * rcv_imag, axis=0)
    scale = 1.0 / jnp.maximum(counts, 1.0)
    stacked = (jnp.concatenate([cross_real, cross_imag], axis=2) * scale[:, :, None]).astype(
        jnp.bfloat16
    )
    src_count, rcv_count = counts.shape
    result = jnp.dot(
        stacked.reshape(src_count * rcv_count, 2 * freq_count),
        lags,
        preferred_element_type=jnp.float32,
    )
    weight = mask_block.astype(jnp.float32)[:, :, None] * (1.0 / math.sqrt(freq_count))
    return result.reshape(src_count, rcv_count, lags.shape[1]) * weight


def shards(traces, window_valid, pair_mask):
    whitened = whiten(traces, window_valid, fourier_table(NS, NF), HALF)
    own_flags = window_valid.astype(jnp.bfloat16)
    sources, source_flags = (
        lax.all_gather(whitened, "rcv", axis=1, tiled=True),
        lax.all_gather(own_flags, "rcv", axis=1, tiled=True),
    )
    src_total = pair_mask.shape[0]
    rcv_total = pair_mask.shape[1]
    everything, all_flags = (
        lax.all_gather(sources, "src", axis=1, tiled=True),
        lax.all_gather(source_flags, "src", axis=1, tiled=True),
    )
    start = lax.axis_index("rcv") * rcv_total
    receivers = lax.dynamic_slice_in_dim(everything, start, rcv_total, 1)
    receiver_flags = lax.dynamic_slice_in_dim(all_flags, start, rcv_total, 1)
    lags = lag_table(NS, NF, LAGS)
    sub_width = 16

    def fill_block(block_index, output):
        start = block_index * sub_width
        receiver_part = lax.dynamic_slice_in_dim(receivers, start, sub_width, 1)
        flag_part = lax.dynamic_slice_in_dim(receiver_flags, start, sub_width, 1)
        mask_part = lax.dynamic_slice_in_dim(pair_mask, start, sub_width, 1)
        values = correlate(sources, receiver_part, source_flags, flag_part, mask_part, lags)
        return lax.dynamic_update_slice_in_dim(output, values, start, 1)

    output = jnp.zeros((src_total, rcv_total, LAGS), jnp.float32)
    return lax.fori_loop(0, rcv_total // sub_width, fill_block, output)


def solution(mesh):
    in_specs = (P(None, ("src", "rcv"), None), P(None, ("src", "rcv")), P("src", "rcv"))
    out_specs = P("src", "rcv", None)
    return jax.shard_map(shards, mesh=mesh, in_specs=in_specs, out_specs=out_specs, check_vma=False)
```

profile of v0, /device:TPU:1, one launch (start us, length us, event | category | flops | bytes accessed | tf_op | source)
XLA Modules:
  0.0 364.3 jit_solution(4943946694667401015)
XLA Ops:
  6.5 0.8 convert_bitcast_fusion
  7.3 0.1 convert_element_type.79
  7.4 0.8 reshape.46
  8.2 78.7 %cosine_convert_fusion = (bf16[3072,1536]{1,0:T(8,128)(2,1)S(1)}, bf16[3072,1536]{1,0:T(8,128)(2,1)S(1)}) fusion(s32[1536]{0:T(1024)S(1)} %iota_add_fusion), kind=kLoop, calls=%fused_computation.28 | loop fusion | flops 56623104 | bytes 18880512 | tf_op jit(solution)/shard_map/convert.2
  86.9 2.5 fusion.21
  89.5 13.6 %reduce_window.7 = f32[8,1536]{1,0:T(8,128)S(1)} reduce-window(f32[8,1536]{1,0:T(8,128)S(1)} %fusion.31, f32[]{:T(128)} %constant.80.clone.1), window={size=1x65 pad=0_0x32_32}, to_apply=%region_0.1 | reduce-window | flops 786432 | bytes 98308 | tf_op jit(solution)/shard_map/reduce_window | solution.py:44
  103.3 24.8 %all_gather.12 = bf16[2,64,3072]{2,0,1:T(2,128)(2,1)} all-gather(bf16[2,4,3072]{2,0,1:T(2,128)(2,1)S(1)} %copy.24), channel_id=1, replica_groups=mesh['src'=16,'rcv'=16] {'rcv'}, dimensions={1}, use_global_device_ids=true | all-gather | bytes 835584 | tf_op jit(solution)/shard_map/all_gather | solution.py:85
  128.0 16.1 %all-gather = bf16[16,4,2]{1,2,0:T(2,128)(2,1)S(1)} all-gather(bf16[1,4,2]{1,2,0:T(2,128)(2,1)S(1)} %get-tuple-element.197), channel_id=1, replica_groups=mesh['src'=16,'rcv'=16] {'rcv'}, dimensions={0}, use_global_device_ids=true | all-gather | bytes 272 | tf_op jit(solution)/shard_map/all_gather | solution.py:86
  144.2 0.1 reshape.49
  144.3 0.1 reshape.50
  144.4 1.3 copy.28
  145.7 36.1 %all-gather.1 = bf16[16,64,2]{1,2,0:T(2,128)(2,1)S(1)} all-gather(bf16[1,64,2]{1,2,0:T(2,128)(2,1)S(1)} %reshape.50), channel_id=1, replica_groups=mesh['src'=16,'rcv'=16] {'src'}, dimensions={0}, use_global_device_ids=true | all-gather | bytes 4352 | tf_op jit(solution)/shard_map/all_gather | solution.py:92
  181.8 0.1 reshape.51
  181.9 0.1 dynamic-slice_bitcast_fusion
  182.0 13.7 %cosine_convert_fusion.1 = (bf16[1536,512]{1,0:T(8,128)(2,1)S(1)}, bf16[1536,512]{1,0:T(8,128)(2,1)S(1)}) fusion(s32[512]{0:T(512)S(1)} %iota_add_fusion.1, s32[1536]{0:T(1024)S(1)} %iota_add_fusion), kind=kLoop, calls=%fused_computation.39 | loop fusion | flops 9437184 | bytes 3153920 | tf_op jit(solution)/shard_map/convert
  195.7 1.8 pad_maximum_fusion
  197.6 108.5 %all-gather.4.cloned.1.call-done = bf16[2,1024,3072]{2,0,1:T(2,128)(2,1)} async-done(((bf16[2,64,3072]{2,0,1:T(2,128)(2,1)}), bf16[2,1024,3072]{2,0,1:T(2,128)(2,1)}) %all-gather.4.cloned.1.call-update) | async-done | bytes 12582928 | tf_op jit(solution)/shard_map/all_gather | solution.py:91
  306.0 1.7 constant_dynamic-slice_fusion.4
  307.7 4.5 %broadcast_in_dim.21 = f32[64,64,512]{2,1,0:T(8,128)} broadcast(f32[]{:T(128)} %constant.80.clone.1), dimensions={} | broadcast | bytes 8388612 | tf_op jit(solution)/shard_map/broadcast_in_dim | solution.py:108
  312.2 45.3 %while.13 = (s32[]{:T(128)}, f32[64,64,512]{2,1,0:T(8,128)}, bf16[2,64,3072]{2,1,0:T(8,128)(2,1)S(1)}, bf16[2,64,3072]{2,0,1:T(2,128)(2,1)S(1)}, bf16[2,64]{1,0:...) while((s32[]{:T(128)}, f32[64,64,512]{2,1,0:T(8,128)}, ...), condition=%wide.region_4.5_spmd, body=%wide.region_1.4_spmd.sunk | while | flops 3253706752 | bytes 48329448 | solution.py:109
  312.2 0.3 fusion.42
  312.4 0.1 copy.38
  312.5 0.1 convert_multiply_fusion.2
  312.6 0.1 constant_dynamic-slice_fusion.8
  312.8 0.2 slice_convert_fusion.3
  313.0 5.8 %add_reduce_fusion.2 = (f32[64,16,1536]{2,1,0:T(8,128)S(1)}, f32[64,16,1536]{2,1,0:T(8,128)S(1)}) fusion(f32[2,16,1536]{2,1,0:T(8,128)S(1)} %get-tuple-element.258, f32[2,64,1536]{2,1,0:T(8,128)S(1)} %get-tuple-element.259, f32[2,16,1536]{2,1,0:T(8,128)S(1)} %get-tuple-element.260, f32[2,64,1536]{2,1,0:T(8,128)S(1)} %get-tuple-element.261), kind=kLoop, calls=%fused_computation.3.clone.1 | loop fusion | flops 22020096 | bytes 14548992 | tf_op jit(solution)/shard_map/while/body/eval_jaxpr/reduce_sum | solution.py:65
  318.8 4.7 %multiply_dynamic-update-slice_fusion.2 = f32[64,64,512]{2,1,0:T(8,128)} fusion(f32[64,64,512]{2,1,0:T(8,128)} %get-tuple-element.278, s32[]{:T(128)S(6)} %select_n.53, bf16[3072,512]{1,0:T(8,128)(2,1)S(1)} %copy-done, f32[64,16,1536]{2,1,0:T(8,128)S(1)} %get-tuple-element.262, f32[64,16,1536]{2,1,0:T(8,128)S(1)} %get-tuple-element.263, ...), kind=kOutput, calls=%fused_computation.7.clone.1 | convolution fusion | flops 3231186944 | bytes 17833988 | tf_op jit(solution)/shard_map/while/body/eval_jaxpr/dot_general | solution.py:72
  323.5 0.3 fusion.42
  323.7 0.1 copy.38
  323.8 0.1 convert_multiply_fusion.2
  323.9 0.1 constant_dynamic-slice_fusion.8
  324.1 0.2 slice_convert_fusion.3
  324.3 5.8 %add_reduce_fusion.2 = (f32[64,16,1536]{2,1,0:T(8,128)S(1)}, f32[64,16,1536]{2,1,0:T(8,128)S(1)}) fusion(f32[2,16,1536]{2,1,0:T(8,128)S(1)} %get-tuple-element.258, f32[2,64,1536]{2,1,0:T(8,128)S(1)} %get-tuple-element.259, f32[2,16,1536]{2,1,0:T(8,128)S(1)} %get-tuple-element.260, f32[2,64,1536]{2,1,0:T(8,128)S(1)} %get-tuple-element.261), kind=kLoop, calls=%fused_computation.3.clone.1 | loop fusion | flops 22020096 | bytes 14548992 | tf_op jit(solution)/shard_map/while/body/eval_jaxpr/reduce_sum | solution.py:65
  330.1 4.7 %multiply_dynamic-update-slice_fusion.2 = f32[64,64,512]{2,1,0:T(8,128)} fusion(f32[64,64,512]{2,1,0:T(8,128)} %get-tuple-element.278, s32[]{:T(128)S(6)} %select_n.53, bf16[3072,512]{1,0:T(8,128)(2,1)S(1)} %copy-done, f32[64,16,1536]{2,1,0:T(8,128)S(1)} %get-tuple-element.262, f32[64,16,1536]{2,1,0:T(8,128)S(1)} %get-tuple-element.263, ...), kind=kOutput, calls=%fused_computation.7.clone.1 | convolution fusion | flops 3231186944 | bytes 17833988 | tf_op jit(solution)/shard_map/while/body/eval_jaxpr/dot_general | solution.py:72
  334.8 0.3 fusion.42
  335.1 0.1 copy.38
  335.2 0.1 convert_multiply_fusion.2
  335.2 0.1 constant_dynamic-slice_fusion.8
  335.4 0.2 slice_convert_fusion.3
  335.6 5.8 %add_reduce_fusion.2 = (f32[64,16,1536]{2,1,0:T(8,128)S(1)}, f32[64,16,1536]{2,1,0:T(8,128)S(1)}) fusion(f32[2,16,1536]{2,1,0:T(8,128)S(1)} %get-tuple-element.258, f32[2,64,1536]{2,1,0:T(8,128)S(1)} %get-tuple-element.259, f32[2,16,1536]{2,1,0:T(8,128)S(1)} %get-tuple-element.260, f32[2,64,1536]{2,1,0:T(8,128)S(1)} %get-tuple-element.261), kind=kLoop, calls=%fused_computation.3.clone.1 | loop fusion | flops 22020096 | bytes 14548992 | tf_op jit(solution)/shard_map/while/body/eval_jaxpr/reduce_sum | solution.py:65
  341.5 4.7 %multiply_dynamic-update-slice_fusion.2 = f32[64,64,512]{2,1,0:T(8,128)} fusion(f32[64,64,512]{2,1,0:T(8,128)} %get-tuple-element.278, s32[]{:T(128)S(6)} %select_n.53, bf16[3072,512]{1,0:T(8,128)(2,1)S(1)} %copy-done, f32[64,16,1536]{2,1,0:T(8,128)S(1)} %get-tuple-element.262, f32[64,16,1536]{2,1,0:T(8,128)S(1)} %get-tuple-element.263, ...), kind=kOutput, calls=%fused_computation.7.clone.1 | convolution fusion | flops 3231186944 | bytes 17833988 | tf_op jit(solution)/shard_map/while/body/eval_jaxpr/dot_general | solution.py:72
  346.1 0.3 fusion.42
  346.4 0.1 copy.38
  346.5 0.1 convert_multiply_fusion.2
  346.6 0.1 constant_dynamic-slice_fusion.8
  346.7 0.2 slice_convert_fusion.3
  346.9 5.8 %add_reduce_fusion.2 = (f32[64,16,1536]{2,1,0:T(8,128)S(1)}, f32[64,16,1536]{2,1,0:T(8,128)S(1)}) fusion(f32[2,16,1536]{2,1,0:T(8,128)S(1)} %get-tuple-element.258, f32[2,64,1536]{2,1,0:T(8,128)S(1)} %get-tuple-element.259, f32[2,16,1536]{2,1,0:T(8,128)S(1)} %get-tuple-element.260, f32[2,64,1536]{2,1,0:T(8,128)S(1)} %get-tuple-element.261), kind=kLoop, calls=%fused_computation.3.clone.1 | loop fusion | flops 22020096 | bytes 14548992 | tf_op jit(solution)/shard_map/while/body/eval_jaxpr/reduce_sum | solution.py:65
  352.8 4.7 %multiply_dynamic-update-slice_fusion.2 = f32[64,64,512]{2,1,0:T(8,128)} fusion(f32[64,64,512]{2,1,0:T(8,128)} %get-tuple-element.278, s32[]{:T(128)S(6)} %select_n.53, bf16[3072,512]{1,0:T(8,128)(2,1)S(1)} %copy-done, f32[64,16,1536]{2,1,0:T(8,128)S(1)} %get-tuple-element.262, f32[64,16,1536]{2,1,0:T(8,128)S(1)} %get-tuple-element.263, ...), kind=kOutput, calls=%fused_computation.7.clone.1 | convolution fusion | flops 3231186944 | bytes 17833988 | tf_op jit(solution)/shard_map/while/body/eval_jaxpr/dot_general | solution.py:72
  (25 shorter events, 0.4 us)
Async XLA Ops:
  6.5 299.5 %all-gather.4.cloned.1.call-start = ((), (), s32[]{:S(2)}) async-start(), calls=%async_computation | async-start | bytes 13369344 | tf_op jit(solution)/shard_map/all_gather | solution.py:91
  195.7 116.5 %copy-start.1 = (s32[64,64]{1,0:T(8,128)S(1)}, s32[64,64]{1,0:T(8,128)}, u32[]{:S(2)}) copy-start(s32[64,64]{1,0:T(8,128)} %param.7) | copy-start | bytes 49156
  312.8 6.0 %copy-start = (bf16[3072,512]{1,0:T(8,128)(2,1)S(1)}, bf16[3072,512]{1,0:T(8,128)(2,1)}, u32[]{:S(2)}) copy-start(bf16[3072,512]{1,0:T(8,128)(2,1)} %get-tuple-element.296) | copy-start | bytes 9437188 | tf_op jit(solution)/shard_map/while
  324.1 6.0 %copy-start = (bf16[3072,512]{1,0:T(8,128)(2,1)S(1)}, bf16[3072,512]{1,0:T(8,128)(2,1)}, u32[]{:S(2)}) copy-start(bf16[3072,512]{1,0:T(8,128)(2,1)} %get-tuple-element.296) | copy-start | bytes 9437188 | tf_op jit(solution)/shard_map/while
  335.4 6.0 %copy-start = (bf16[3072,512]{1,0:T(8,128)(2,1)S(1)}, bf16[3072,512]{1,0:T(8,128)(2,1)}, u32[]{:S(2)}) copy-start(bf16[3072,512]{1,0:T(8,128)(2,1)} %get-tuple-element.296) | copy-start | bytes 9437188 | tf_op jit(solution)/shard_map/while
  346.7 6.0 %copy-start = (bf16[3072,512]{1,0:T(8,128)(2,1)S(1)}, bf16[3072,512]{1,0:T(8,128)(2,1)}, u32[]{:S(2)}) copy-start(bf16[3072,512]{1,0:T(8,128)(2,1)} %get-tuple-element.296) | copy-start | bytes 9437188 | tf_op jit(solution)/shard_map/while
Sparse Core Ops, SparseCore 0:
  128.2 177.8 all-gather.3
where the time goes:
time: 365 us; the launch traced here: 364 us
  other arithmetic  133 us (36%)
  waiting for transfers between devices  108 us (30%)
  blocking collectives  77 us (21%)
  matrix products  22.2 us (6%)
  between operations  13.5 us (4%)
  local copies, waits for them, and re-layouts  9.69 us (3%)
    all_gather x1, waiting for transfers between devices, shards(): lax.all_gather(sources, 'src', axis=1, tiled=True)  108 us
    another operation x2, other arithmetic  92.5 us
    all_gather x1, blocking collectives, shards(): lax.all_gather(source_flags, 'src', axis=1, tiled=True)  36.1 us
    all_gather x1, blocking collectives, shards(): lax.all_gather(whitened, 'rcv', axis=1, tiled=True)  24.8 us
    reduce_sum x4, other arithmetic, correlate(): cross_real = jnp.sum(src_real * rcv_real + src_imag * rcv_imag, axis=0)  23.3 us
    dot_general x4, matrix products, correlate(): jnp.dot(stacked.reshape(src_count * rcv_count, 2 * freq_count), lags, pre...  18.7 us
    all_gather x1, blocking collectives, shards(): lax.all_gather(own_flags, 'rcv', axis=1, tiled=True)  16.1 us
    another operation x1, other arithmetic, whiten(): lax.reduce_window(amplitude, jnp.zeros((), amplitude.dtype), lax.add, (1,...  13.6 us
  transfers between devices with their start and end apart: 1, of which 1 were waited for; matrix products, arithmetic and copies ran while one was open for 5% of the time, Pallas kernels for 0%

commit v1 on v0

v1 whole, which is shorter than its diff:
```python
import functools
import math

import jax
import jax.numpy as jnp
import numpy as np
from jax import lax
from jax.experimental import pallas as pl
from jax.experimental.pallas import tpu as pltpu
from jax.sharding import PartitionSpec as P

NS = 3072
NF = 1536
LAGS = 512
HALF = 32
WIN = 2
EPSILON = 1e-06
STEP = 2.0 * math.pi / NS
INVALID = 100.0
F32 = jnp.float32
BF16 = jnp.bfloat16
VMEM = pl.BlockSpec(memory_space=pltpu.VMEM)


def cos_sin(angles):
    return np.stack([np.cos(angles), np.sin(angles)]).astype(np.float32)


def seeds():
    freqs = np.arange(1, NF + 1, dtype=np.float64) * STEP
    halves = np.arange(LAGS // 2, dtype=np.float64) + 0.5
    first = cos_sin(np.arange(16)[:, None] * freqs[None, :])
    turn = cos_sin(np.broadcast_to(16 * freqs, (8, NF)))
    phase = cos_sin(np.broadcast_to(0.5 * freqs, (8, NF)))
    lag_first = cos_sin(freqs[:16, None] * halves[None, :])
    lag_turn = cos_sin(np.broadcast_to(16 * STEP * halves, (8, LAGS // 2)))
    return first, turn, phase, lag_first, lag_turn


def rotate(cosine, sine, turn_cos, turn_sin):
    return cosine * turn_cos - sine * turn_sin, sine * turn_cos + cosine * turn_sin


def fill_forward(first_ref, turn_ref, table):
    width = 512
    for block in range(NF // width):
        lanes = pl.ds(block * width, width)
        imag_lanes = pl.ds(NF + block * width, width)
        turn_cos, turn_sin = turn_ref[0, 0:1, lanes], turn_ref[1, 0:1, lanes]

        def rows(index, held):
            cosine, sine = held
            at = pl.ds(pl.multiple_of(index * 16, 16), 16)
            table[at, lanes] = cosine.astype(BF16)
            table[at, imag_lanes] = (-sine).astype(BF16)
            return rotate(cosine, sine, turn_cos, turn_sin)

        lax.fori_loop(0, NS // 32, rows, (first_ref[0, :, lanes], first_ref[1, :, lanes]))


def fill_lags(first_ref, turn_ref, cos_table, sin_table):
    turn_cos, turn_sin = turn_ref[0, 0:1, :], turn_ref[1, 0:1, :]

    def rows(index, held):
        cosine, sine = held
        at = pl.ds(pl.multiple_of(index * 16, 16), 16)
        cos_table[at, :] = cosine.astype(BF16)
        sin_table[at, :] = sine.astype(BF16)
        return rotate(cosine, sine, turn_cos, turn_sin)

    lax.fori_loop(0, NF // 16, rows, (first_ref[0], first_ref[1]))


def whiten_kernel(
    count, pieces_ref, first_ref, turn_ref, phase_ref, lag_first_ref, lag_turn_ref,
    src_ref, rcv_ref, flags_ref, cos_ref, sin_ref, table, ordered, left, spectrum, high, low
):
    half = count // 2
    fill_forward(first_ref, turn_ref, table)
    fill_lags(lag_first_ref, lag_turn_ref, cos_ref, sin_ref)
    for piece in range(count // 4):
        rows = pieces_ref[piece].astype(F32)
        for part in range(4):
            ordered[part, 4 * piece : 4 * piece + 4, :] = rows[4 * part : 4 * part + 4]
    lane = lax.broadcasted_iota(jnp.int32, (count, 128), 1)
    flags = jnp.zeros((count, 128), F32)
    for window in range(WIN):
        valid = ordered[window, :, 0:1] < 0.5 * INVALID
        flags = jnp.where((lane == window) & valid, 1.0, flags)
        for part in (window, WIN + window):
            left[pl.ds(part * count, count), :] = jnp.where(valid, ordered[part], 0.0).astype(BF16)
    flags_ref[...] = flags
    total = WIN * count
    width = 256
    even = lax.broadcasted_iota(jnp.int32, (1, width), 1) % 2 == 0
    for ref in (high, low):
        ref[:, 0:128] = jnp.zeros((total, 128), BF16)
        ref[:, 128 + NF : 256 + NF] = jnp.zeros((total, 128), BF16)

    def transform(block, carry):
        at = pl.multiple_of(block * width, width)
        square = None
        for base in (0, NF):
            lanes = pl.ds(pl.multiple_of(base + at, width), width)
            both = jnp.dot(left[...], table[:, lanes], preferred_element_type=F32)
            later = both[total:]
            value = both[:total] + jnp.where(even, -later, later)
            spectrum[:, lanes] = value
            square = value * value if square is None else square + value * value
        amplitude = jnp.sqrt(square)
        rounded = amplitude.astype(BF16)
        lanes = pl.ds(pl.multiple_of(128 + at, 128), width)
        high[:, lanes] = rounded
        low[:, lanes] = (amplitude - rounded.astype(F32)).astype(BF16)
        return carry

    lax.fori_loop(0, NF // width, transform, 0)
    offset = lax.broadcasted_iota(jnp.int32, (2 * width, width), 0) - lax.broadcasted_iota(
        jnp.int32, (2 * width, width), 1
    )
    band = jnp.where((offset >= 128 - HALF) & (offset <= 128 + HALF), 1.0, 0.0).astype(BF16)

    def smooth(block, carry):
        at = pl.multiple_of(block * width, width)
        around = pl.ds(at, 2 * width)
        running = jnp.dot(high[:, around], band, preferred_element_type=F32)
        running += jnp.dot(low[:, around], band, preferred_element_type=F32)
        factor = 1.0 / (running * (1.0 / (2 * HALF + 1)) + EPSILON)
        real_lanes = pl.ds(at, width)
        imag_lanes = pl.ds(pl.multiple_of(NF + at, width), width)
        real = (spectrum[:, real_lanes] * factor).astype(BF16)
        imag = (spectrum[:, imag_lanes] * factor).astype(BF16)
        turn_cos, turn_sin = phase_ref[0, 0:1, real_lanes], phase_ref[1, 0:1, real_lanes]
        for window in range(WIN):
            start = window * count
            src_real = real[start : start + half].astype(F32)
            src_imag = imag[start : start + half].astype(F32)
            src_ref[window, :, real_lanes] = src_real * turn_cos + src_imag * turn_sin
            src_ref[window, :, imag_lanes] = src_imag * turn_cos - src_real * turn_sin
            rcv_ref[window, :, real_lanes] = real[start + half : start + count]
            rcv_ref[window, :, imag_lanes] = imag[start + half : start + count]
        return carry

    lax.fori_loop(0, NF // width, smooth, 0)


def whitened(pieces):
    first, turn, phase, lag_first, lag_turn = seeds()
    count = pieces.shape[0] * 4
    half = count // 2
    return pl.pallas_call(
        functools.partial(whiten_kernel, count),
        out_shape=[
            jax.ShapeDtypeStruct((WIN, half, NS), F32),
            jax.ShapeDtypeStruct((WIN, half, NS), BF16),
            jax.ShapeDtypeStruct((count, 128), F32),
            jax.ShapeDtypeStruct((NF, LAGS // 2), BF16),
            jax.ShapeDtypeStruct((NF, LAGS // 2), BF16),
        ],
        in_specs=[VMEM] * 6,
        out_specs=[VMEM] * 5,
        scratch_shapes=[
            pltpu.VMEM((NS // 2, NS), BF16),
            pltpu.VMEM((4, count, NS // 2), F32),
            pltpu.VMEM((4 * count, NS // 2), BF16),
            pltpu.VMEM((WIN * count, NS), F32),
            pltpu.VMEM((WIN * count, NF + 256), BF16),
            pltpu.VMEM((WIN * count, NF + 256), BF16),
        ],
        compiler_params=pltpu.CompilerParams(vmem_limit_bytes=56 * 2**20),
    )(pieces, first, turn, phase, lag_first, lag_turn)


CHUNK = 4


def correlate_kernel(steps, src_ref, rcv_ref, flags_ref, mask_ref, cos_ref, sin_ref, out_ref,
                     weights, real_a, imag_a, real_b, imag_b):
    step = pl.program_id(0)
    half = rcv_ref.shape[1]
    rows = CHUNK * half
    groups = half // 16

    @pl.when(step == 0)
    def _():
        counts = lax.dot_general(
            flags_ref[half:, :].astype(BF16), flags_ref[:half, :].astype(BF16),
            (((1,), (1,)), ((), ())), preferred_element_type=F32)
        by_receiver = mask_ref[...].astype(F32).T
        weights[:, :half] = by_receiver * (1.0 / math.sqrt(NF)) / jnp.maximum(counts, 1.0)

    def cross(real_buf, imag_buf, inside):
        eight = lax.div(jnp.minimum(step, steps - 1) * CHUNK, 8)
        for block in range(NF // 128):
            real_lanes = slice(block * 128, block * 128 + 128)
            imag_lanes = slice(NF + block * 128, NF + block * 128 + 128)
            received = [
                [
                    (rcv_ref[w, 16 * g : 16 * g + 16, real_lanes], rcv_ref[w, 16 * g : 16 * g + 16, imag_lanes])
                    for w in range(WIN)
                ]
                for g in range(groups)
            ]
            for source in range(CHUNK):
                at = slice(inside + source, inside + source + 1)
                sent = [
                    tuple(
                        jnp.broadcast_to(src_ref[w, eight, at, lanes], (16, 128)).astype(BF16)
                        for lanes in (real_lanes, imag_lanes)
                    )
                    for w in range(WIN)
                ]
                for g in range(groups):
                    real = imag = None
                    for w in range(WIN):
                        (ar, ai), (br, bi) = sent[w], received[g][w]
                        more_real = ar * br + ai * bi
                        more_imag = ai * br - ar * bi
                        real = more_real if real is None else real + more_real
                        imag = more_imag if imag is None else imag + more_imag
                    place = slice(source * half + 16 * g, source * half + 16 * g + 16)
                    real_buf[place, real_lanes] = real
                    imag_buf[place, real_lanes] = imag

    def lags(real_buf, imag_buf):
        width = LAGS // 2
        even = jnp.dot(real_buf[...], cos_ref[...], preferred_element_type=F32)
        odd = jnp.dot(imag_buf[...], sin_ref[...], preferred_element_type=F32)
        first = jnp.maximum(step - 1, 0) * CHUNK
        near = pltpu.roll(weights[...], lax.rem(128 - first, 128), 1)
        back = 127 - lax.broadcasted_iota(jnp.int32, (half, 128), 1)
        for source in range(CHUNK):
            place = slice(source * half, source * half + half)
            weight = jnp.broadcast_to(near[:, source : source + 1], (half, 128))
            for block in range(width // 128):
                lanes = slice(block * 128, block * 128 + 128)
                e, o = even[place, lanes], odd[place, lanes]
                out_ref[source, :, width + block * 128 : width + block * 128 + 128] = (e - o) * weight
                flipped = jnp.take_along_axis((e + o) * weight, back, axis=1)
                out_ref[source, :, width - block * 128 - 128 : width - block * 128] = flipped

    @pl.when(step % 2 == 0)
    def _():
        lags(real_b, imag_b)
        cross(real_a, imag_a, 0)

    @pl.when(step % 2 == 1)
    def _():
        lags(real_a, imag_a)
        cross(real_b, imag_b, CHUNK % 8)


def correlated(src, rcv, flags, mask, cos_table, sin_table):
    half = rcv.shape[1]
    steps = half // CHUNK
    whole = lambda a: pl.BlockSpec(a.shape, lambda s: (0,) * a.ndim, pipeline_mode=pl.Buffered(1))
    args = (src.reshape(WIN, half // 8, 8, NS), rcv, flags, mask, cos_table, sin_table)
    buffers = [pltpu.VMEM((CHUNK * half, NF), BF16)] * 4
    return pl.pallas_call(
        functools.partial(correlate_kernel, steps),
        grid=(steps + 1,),
        out_shape=jax.ShapeDtypeStruct((half, half, LAGS), F32),
        in_specs=[whole(a) for a in args],
        out_specs=pl.BlockSpec((CHUNK, half, LAGS), lambda s: (jnp.maximum(s - 1, 0), 0, 0)),
        scratch_shapes=[pltpu.VMEM((half, 128), F32)] + buffers,
        compiler_params=pltpu.CompilerParams(vmem_limit_bytes=48 * 2**20),
    )(*args)

MESH = pl.DeviceIdType.MESH


def gather_kernel(side, mine_ref, out_ref, send_sems, recv_sems):
    s, r = lax.axis_index("src"), lax.axis_index("rcv")
    barrier = pltpu.get_barrier_semaphore()

    def greet_row(k, carry):
        pl.semaphore_signal(barrier, inc=1, device_id=(s, lax.rem(r + k, side)), device_id_type=MESH)
        return carry

    def greet_senders(k, carry):
        pl.semaphore_signal(barrier, inc=1, device_id=(r, lax.rem(s + k, side)), device_id_type=MESH)
        return carry

    lax.fori_loop(1, side, greet_row, 0)
    lax.fori_loop(1, side, greet_senders, 0)

    @pl.when(s != r)
    def _():
        pl.semaphore_signal(barrier, inc=1, device_id=(r, s), device_id_type=MESH)

    pl.semaphore_wait(barrier, 2 * (side - 1) + jnp.where(s == r, 0, 1))

    def column(k):
        return pltpu.make_async_remote_copy(
            src_ref=mine_ref, dst_ref=out_ref.at[side + r],
            send_sem=send_sems.at[1], recv_sem=recv_sems.at[1],
            device_id=(lax.rem(s + k, side), s), device_id_type=MESH)

    def row(k):
        return pltpu.make_async_remote_copy(
            src_ref=mine_ref, dst_ref=out_ref.at[r],
            send_sem=send_sems.at[0], recv_sem=recv_sems.at[0],
            device_id=(s, lax.rem(r + k, side)), device_id_type=MESH)

    def send(k, carry):
        column(k).start()
        row(k).start()
        return carry

    own = pltpu.make_async_copy(mine_ref, out_ref.at[r], recv_sems.at[0])
    own.start()
    lax.fori_loop(1, side, send, 0)
    first = pltpu.make_async_remote_copy(
        src_ref=mine_ref, dst_ref=out_ref.at[side + r],
        send_sem=send_sems.at[2], recv_sem=recv_sems.at[1],
        device_id=(s, s), device_id_type=MESH)

    @pl.when(s != r)
    def _():
        first.start()

    @pl.when(s == r)
    def _():
        pltpu.make_async_copy(mine_ref, out_ref.at[side + r], recv_sems.at[1]).start()

    for half in range(2):
        block = out_ref.at[pl.ds(half * side, side)]
        pltpu.make_async_copy(block, block, recv_sems.at[half]).wait()
        block = out_ref.at[pl.ds(0, side - 1)]
        pltpu.make_async_copy(block, block, send_sems.at[half]).wait()

    @pl.when(s != r)
    def _():
        first.wait_send()


def gathered(side, mine):
    return pl.pallas_call(
        functools.partial(gather_kernel, side),
        out_shape=jax.ShapeDtypeStruct((2 * side,) + mine.shape, mine.dtype),
        in_specs=[VMEM],
        out_specs=VMEM,
        scratch_shapes=[pltpu.SemaphoreType.DMA((3,)), pltpu.SemaphoreType.DMA((2,))],
        compiler_params=pltpu.CompilerParams(collective_id=0, has_side_effects=True),
    )(mine)


def shards(side, traces, window_valid, pair_mask):
    marked = jnp.where(window_valid[:, :, None] != 0, traces, jnp.asarray(INVALID, traces.dtype))
    windows, channels, samples = traces.shape
    mine = marked.reshape(windows, channels, 2, samples // 2).transpose(2, 0, 1, 3)
    mine = mine.reshape(2 * windows * channels, samples // 2)
    pieces = gathered(side, mine)
    src, rcv, flags, cos_table, sin_table = whitened(pieces)
    return correlated(src, rcv, flags, pair_mask, cos_table, sin_table)


def solution(mesh):
    in_specs = (P(None, ("src", "rcv"), None), P(None, ("src", "rcv")), P("src", "rcv"))
    return jax.shard_map(
        functools.partial(shards, mesh.shape["src"]),
        mesh=mesh, in_specs=in_specs, out_specs=P("src", "rcv", None), check_vma=False)
```

time: 365 us -> 83.6 us (0.23)
  the two profiles are of different devices: /device:TPU:1 before, /device:TPU:41 now
where the time goes in v1:
time: 83.6 us; the launch traced here: 83.1 us
  Pallas kernels  75.2 us (90%)
  local copies, waits for them, and re-layouts  6.31 us (8%)
  other arithmetic  1.57 us (2%)
    pallas_call x1, Pallas kernels, gathered(): pl.pallas_call(functools.partial(gather_kernel, side), out_shape=jax.Shap...  38.1 us
    pallas_call x1, Pallas kernels, correlated(): pl.pallas_call(functools.partial(correlate_kernel, steps), grid=(steps +...  20.5 us
    pallas_call x1, Pallas kernels, whitened(): pl.pallas_call(functools.partial(whiten_kernel, count), out_shape=[jax.Sh...  16.6 us
    unnamed x12, local copies, waits for them, and re-layouts  5.65 us

profile of v1, /device:TPU:41, one launch (start us, length us, event | category | flops | bytes accessed | tf_op | source)
XLA Modules:
  0.0 83.1 jit_solution(2833320572218548268)
XLA Ops:
  0.0 0.7 broadcast_compare_fusion
  0.7 0.9 %broadcast_select_fusion = bf16[2,4,3072]{2,1,0:T(4,128)(2,1)S(1)} fusion(bf16[2,4,3072]{2,1,0:T(4,128)(2,1)} %param.8, pred[2,4]{1,0:T(4,128)(4,1)S(1)} %broadcast_compare_fusion), kind=kLoop, calls=%fused_computation.1 | loop fusion | flops 24576 | bytes 98312 | tf_op jit(solution)/shard_map/jit(_where)/select_n | solution.py:349
  1.6 0.6 reshape.12.mine_ref
  2.2 0.0 copy-start.5
  2.2 38.1 %shard_map.82.pieces_ref = bf16[32,16,1536]{2,1,0:T(8,128)(2,1)} custom-call(bf16[16,1536]{1,0:T(8,128)(2,1)} %reshape.12.mine_ref), custom_call_target="tpu_custom_call" | custom-call | tf_op jit(solution)/shard_map/pallas_call | solution.py:338
  40.3 16.6 %shard_map.83 = (f32[2,64,3072]{2,1,0:T(8,128)}, bf16[2,64,3072]{2,1,0:T(8,128)(2,1)}, f32[128,128]{1,0:T(8,128)}, bf16[1536,256]{1,0:T(8,128)(2,1)}, bf16[1536,256]{1,0:T(8,128)(2,1)}) custom-call(bf16[32,16,1536]{2,1,0:T(8,128)(2,1)} %shard_map.82.pieces_ref, f32[2,16,1536]{2,1,0:T(8,128)} %constant.14.clone.first_ref, ...), custom_call_target="tpu_custom_call" | custom-call | tf_op jit(solution)/shard_map/pallas_call | solution.py:151
  56.9 0.0 copy-done.5
  56.9 0.0 copy-start
  56.9 1.4 %copy-done = f32[2,64,3072]{2,1,0:T(8,128)S(1)} copy-done((f32[2,64,3072]{2,1,0:T(8,128)S(1)}, f32[2,64,3072]{2,1,0:T(8,128)}, u32[]{:S(2)}) %copy-start) | copy-done | bytes 1572888
  58.4 0.0 copy-start.1
  58.4 1.1 %copy-done.1 = bf16[2,64,3072]{2,1,0:T(8,128)(2,1)S(1)} copy-done((bf16[2,64,3072]{2,1,0:T(8,128)(2,1)S(1)}, bf16[2,64,3072]{2,1,0:T(8,128)(2,1)}, u32[]{:S(2)}) %copy-start.1) | copy-done | bytes 786456
  59.5 0.0 copy-start.2
  59.5 1.1 %copy-done.2 = bf16[1536,256]{1,0:T(8,128)(2,1)S(1)} copy-done((bf16[1536,256]{1,0:T(8,128)(2,1)S(1)}, bf16[1536,256]{1,0:T(8,128)(2,1)}, u32[]{:S(2)}) %copy-start.2) | copy-done | bytes 786456
  60.6 0.0 copy-start.3
  60.6 1.1 %copy-done.3 = bf16[1536,256]{1,0:T(8,128)(2,1)S(1)} copy-done((bf16[1536,256]{1,0:T(8,128)(2,1)S(1)}, bf16[1536,256]{1,0:T(8,128)(2,1)}, u32[]{:S(2)}) %copy-start.3) | copy-done | bytes 786456
  61.8 0.0 copy-start.4
  61.8 0.8 %copy-done.4 = f32[128,128]{1,0:T(8,128)S(1)} copy-done((f32[128,128]{1,0:T(8,128)S(1)}, f32[128,128]{1,0:T(8,128)}, u32[]{:S(2)}) %copy-start.4) | copy-done | bytes 65560
  62.6 20.5 %shard_map.84 = f32[64,64,512]{2,1,0:T(8,128)} custom-call(f32[2,8,8,3072]{3,2,1,0:T(8,128)S(1)} %bitcast.8, bf16[2,64,3072]{2,1,0:T(8,128)(2,1)S(1)} %copy-done.1, f32[128,128]{1,0:T(8,128)S(1)} %copy-done.4, s32[64,64]{1,0:T(8,128)S(1)} %copy-done.5, bf16[1536,256]{1,0:T(8,128)(2,1)S(1)} %copy-done.2, bf16[1536,256]{1,0:T(8,128)(2,1)S(1)} %copy-done.3), custom_call_target="tpu_custom_call" | custom-call | tf_op jit(solution)/shard_map/pallas_call | solution.py:259
  (1 shorter events, 0.0 us)
Async XLA Ops:
  2.2 54.7 %copy-start.5 = (s32[64,64]{1,0:T(8,128)S(1)}, s32[64,64]{1,0:T(8,128)}, u32[]{:S(2)}) copy-start(s32[64,64]{1,0:T(8,128)} %mask_ref.1) | copy-start | bytes 49156
  56.9 1.4 %copy-start = (f32[2,64,3072]{2,1,0:T(8,128)S(1)}, f32[2,64,3072]{2,1,0:T(8,128)}, u32[]{:S(2)}) copy-start(f32[2,64,3072]{2,1,0:T(8,128)} %get-tuple-element.10) | copy-start | bytes 4718596
  58.4 1.1 %copy-start.1 = (bf16[2,64,3072]{2,1,0:T(8,128)(2,1)S(1)}, bf16[2,64,3072]{2,1,0:T(8,128)(2,1)}, u32[]{:S(2)}) copy-start(bf16[2,64,3072]{2,1,0:T(8,128)(2,1)} %get-tuple-element.11.rcv_ref) | copy-start | bytes 2359300
  59.5 1.1 %copy-start.2 = (bf16[1536,256]{1,0:T(8,128)(2,1)S(1)}, bf16[1536,256]{1,0:T(8,128)(2,1)}, u32[]{:S(2)}) copy-start(bf16[1536,256]{1,0:T(8,128)(2,1)} %get-tuple-element.13.cos_ref) | copy-start | bytes 2359300
  60.6 1.1 %copy-start.3 = (bf16[1536,256]{1,0:T(8,128)(2,1)S(1)}, bf16[1536,256]{1,0:T(8,128)(2,1)}, u32[]{:S(2)}) copy-start(bf16[1536,256]{1,0:T(8,128)(2,1)} %get-tuple-element.14.sin_ref) | copy-start | bytes 2359300
  61.8 0.8 %copy-start.4 = (f32[128,128]{1,0:T(8,128)S(1)}, f32[128,128]{1,0:T(8,128)}, u32[]{:S(2)}) copy-start(f32[128,128]{1,0:T(8,128)} %get-tuple-element.12.flags_ref) | copy-start | bytes 196612

commit v2 on v1

v2 whole, which is shorter than its diff:
```python
import functools
import math

import jax
import jax.numpy as jnp
import numpy as np
from jax import lax
from jax.experimental import pallas as pl
from jax.experimental.pallas import tpu as pltpu
from jax.sharding import PartitionSpec as P

NS = 3072
NF = 1536
LAGS = 512
HALF = 32
WIN = 2
EPSILON = 1e-06
STEP = 2.0 * math.pi / NS
INVALID = 100.0
F32 = jnp.float32
BF16 = jnp.bfloat16
VMEM = pl.BlockSpec(memory_space=pltpu.VMEM)


def cos_sin(angles):
    return np.stack([np.cos(angles), np.sin(angles)]).astype(np.float32)


def seeds():
    freqs = np.arange(1, NF + 1, dtype=np.float64) * STEP
    halves = np.arange(LAGS // 2, dtype=np.float64) + 0.5
    first = cos_sin(np.arange(16)[:, None] * freqs[None, :])
    turn = cos_sin(np.broadcast_to(16 * freqs, (8, NF)))
    phase = cos_sin(np.broadcast_to(0.5 * freqs, (8, NF)))
    lag_first = cos_sin(freqs[:16, None] * halves[None, :])
    lag_turn = cos_sin(np.broadcast_to(16 * STEP * halves, (8, LAGS // 2)))
    return first, turn, phase, lag_first, lag_turn


def rotate(cosine, sine, turn_cos, turn_sin):
    return cosine * turn_cos - sine * turn_sin, sine * turn_cos + cosine * turn_sin


def fill_forward(first_ref, turn_ref, table, block, width):
    lanes = pl.ds(block * width, width)
    imag_lanes = pl.ds(NF + block * width, width)
    turn_cos, turn_sin = turn_ref[0, 0:1, lanes], turn_ref[1, 0:1, lanes]

    def rows(index, held):
        cosine, sine = held
        at = pl.ds(pl.multiple_of(index * 16, 16), 16)
        table[at, lanes] = cosine.astype(BF16)
        table[at, imag_lanes] = (-sine).astype(BF16)
        return rotate(cosine, sine, turn_cos, turn_sin)

    lax.fori_loop(0, NS // 32, rows, (first_ref[0, :, lanes], first_ref[1, :, lanes]))


def fill_lags(first_ref, turn_ref, cos_table, sin_table):
    turn_cos, turn_sin = turn_ref[0, 0:1, :], turn_ref[1, 0:1, :]

    def rows(index, held):
        cosine, sine = held
        at = pl.ds(pl.multiple_of(index * 16, 16), 16)
        cos_table[at, :] = cosine.astype(BF16)
        sin_table[at, :] = sine.astype(BF16)
        return rotate(cosine, sine, turn_cos, turn_sin)

    lax.fori_loop(0, NF // 16, rows, (first_ref[0], first_ref[1]))


def channel_group(slot):
    if slot < 16:
        core, low, y = slot // 8, slot // 4 % 2, slot % 4
        return 8 * low + 2 * y + core
    return 16 + slot % 8 * 2 + (slot - 16) // 8


def whiten_kernel(
    count, pieces_ref, table, phase_ref, src_ref, rcv_ref, flags_ref, ordered, left, spectrum, high, low
):
    half = count // 2
    for piece in range(count // 4):
        rows = pieces_ref[piece].astype(F32)
        first = 4 * channel_group(piece)
        for part in range(4):
            ordered[part, first : first + 4, :] = rows[4 * part : 4 * part + 4]
    lane = lax.broadcasted_iota(jnp.int32, (count, 128), 1)
    flags = jnp.zeros((count, 128), F32)
    for window in range(WIN):
        valid = ordered[window, :, 0:1] < 0.5 * INVALID
        flags = jnp.where((lane == window) & valid, 1.0, flags)
        for part in (window, WIN + window):
            left[pl.ds(part * count, count), :] = jnp.where(valid, ordered[part], 0.0).astype(BF16)
    flags_ref[...] = flags
    total = WIN * count
    width = 256
    even = lax.broadcasted_iota(jnp.int32, (1, width), 1) % 2 == 0
    for ref in (high, low):
        ref[:, 0:128] = jnp.zeros((total, 128), BF16)
        ref[:, 128 + NF : 256 + NF] = jnp.zeros((total, 128), BF16)

    def transform(block, carry):
        at = pl.multiple_of(block * width, width)
        square = None
        for base in (0, NF):
            lanes = pl.ds(pl.multiple_of(base + at, width), width)
            both = jnp.dot(left[...], table[:, lanes], preferred_element_type=F32)
            later = both[total:]
            value = both[:total] + jnp.where(even, -later, later)
            spectrum[:, lanes] = value
            square = value * value if square is None else square + value * value
        amplitude = jnp.sqrt(square)
        rounded = amplitude.astype(BF16)
        lanes = pl.ds(pl.multiple_of(128 + at, 128), width)
        high[:, lanes] = rounded
        low[:, lanes] = (amplitude - rounded.astype(F32)).astype(BF16)
        return carry

    lax.fori_loop(0, NF // width, transform, 0)
    offset = lax.broadcasted_iota(jnp.int32, (2 * width, width), 0) - lax.broadcasted_iota(
        jnp.int32, (2 * width, width), 1
    )
    band = jnp.where((offset >= 128 - HALF) & (offset <= 128 + HALF), 1.0, 0.0).astype(BF16)

    def smooth(block, carry):
        at = pl.multiple_of(block * width, width)
        around = pl.ds(at, 2 * width)
        running = jnp.dot(high[:, around], band, preferred_element_type=F32)
        running += jnp.dot(low[:, around], band, preferred_element_type=F32)
        factor = 1.0 / (running * (1.0 / (2 * HALF + 1)) + EPSILON)
        real_lanes = pl.ds(at, width)
        imag_lanes = pl.ds(pl.multiple_of(NF + at, width), width)
        real = (spectrum[:, real_lanes] * factor).astype(BF16)
        imag = (spectrum[:, imag_lanes] * factor).astype(BF16)
        turn_cos, turn_sin = phase_ref[0, 0:1, real_lanes], phase_ref[1, 0:1, real_lanes]
        for window in range(WIN):
            start = window * count
            src_real = real[start : start + half].astype(F32)
            src_imag = imag[start : start + half].astype(F32)
            src_ref[window, :, real_lanes] = src_real * turn_cos + src_imag * turn_sin
            src_ref[window, :, imag_lanes] = src_imag * turn_cos - src_real * turn_sin
            rcv_ref[window, :, real_lanes] = real[start + half : start + count]
            rcv_ref[window, :, imag_lanes] = imag[start + half : start + count]
        return carry

    lax.fori_loop(0, NF // width, smooth, 0)


def whitened(pieces, table, phase):
    count = pieces.shape[0] * 4
    half = count // 2
    return pl.pallas_call(
        functools.partial(whiten_kernel, count),
        out_shape=[
            jax.ShapeDtypeStruct((WIN, half, NS), F32),
            jax.ShapeDtypeStruct((WIN, half, NS), BF16),
            jax.ShapeDtypeStruct((count, 128), F32),
        ],
        in_specs=[VMEM] * 3,
        out_specs=[VMEM] * 3,
        scratch_shapes=[
            pltpu.VMEM((4, count, NS // 2), F32),
            pltpu.VMEM((4 * count, NS // 2), BF16),
            pltpu.VMEM((WIN * count, NS), F32),
            pltpu.VMEM((WIN * count, NF + 256), BF16),
            pltpu.VMEM((WIN * count, NF + 256), BF16),
        ],
        compiler_params=pltpu.CompilerParams(vmem_limit_bytes=18 * 2**20),
    )(pieces, table, phase)


CHUNK = 8
WIDE = 256


def correlate_kernel(src_ref, rcv_ref, flags_ref, mask_ref, cos_ref, sin_ref, out_ref,
                     weights, staged, out_sems):
    half = rcv_ref.shape[1]
    steps = half // CHUNK
    groups = half // 16
    blocks = NF // WIDE

    across = flags_ref[:half, :].T
    counts = sum(flags_ref[half:, w : w + 1] * across[w : w + 1, :] for w in range(WIN))
    by_receiver = mask_ref[...].astype(F32).T
    weights[:, :half] = by_receiver * (1.0 / math.sqrt(NF)) / jnp.maximum(counts, 1.0)
    weights[:, half:] = jnp.zeros((half, 128 - half), F32)
    back = 127 - lax.broadcasted_iota(jnp.int32, (half, 128), 1)

    def finish(even_acc, odd_acc, near, source, slot):
        even, odd = pltpu.matmul_pop(even_acc), pltpu.matmul_pop(odd_acc)
        weight = jnp.broadcast_to(near[:, source : source + 1], (half, 128))
        width = LAGS // 2
        for block in range(width // 128):
            lanes = slice(block * 128, block * 128 + 128)
            e, o = even[:, lanes], odd[:, lanes]
            staged[slot, source, :, width + block * 128 : width + block * 128 + 128] = (e - o) * weight
            flipped = jnp.take_along_axis((e + o) * weight, back, axis=1)
            staged[slot, source, :, width - block * 128 - 128 : width - block * 128] = flipped

    def cross(eight, inside, block):
        real_rows, imag_rows = [], []
        halves = []
        for part in range(WIDE // 128):
            first = block * WIDE + part * 128
            lanes = (slice(first, first + 128), slice(NF + first, NF + first + 128))
            sent = [
                [
                    jnp.broadcast_to(src_ref[w, eight, inside : inside + 1, at], (16, 128)).astype(BF16)
                    for at in lanes
                ]
                for w in range(WIN)
            ]
            halves.append((lanes, sent))
        for g in range(groups):
            reals, imags = [], []
            for lanes, sent in halves:
                real = imag = None
                for w in range(WIN):
                    ar, ai = sent[w]
                    br, bi = (rcv_ref[w, 16 * g : 16 * g + 16, at] for at in lanes)
                    more_real = ar * br + ai * bi
                    more_imag = ai * br - ar * bi
                    real = more_real if real is None else real + more_real
                    imag = more_imag if imag is None else imag + more_imag
                reals.append(real)
                imags.append(imag)
            real_rows.append(jnp.concatenate(reals, axis=1))
            imag_rows.append(jnp.concatenate(imags, axis=1))
        return jnp.concatenate(real_rows, axis=0), jnp.concatenate(imag_rows, axis=0)

    def near_of(chunk):
        return pltpu.roll(weights[...], lax.rem(256 - chunk * CHUNK, 128), 1)

    def put(chunk):
        slot = chunk % 2 if isinstance(chunk, int) else lax.rem(chunk, 2)
        at = pl.ds(pl.multiple_of(chunk * CHUNK, CHUNK), CHUNK)
        return pltpu.make_async_copy(staged.at[slot], out_ref.at[at], out_sems.at[slot])

    def with_accumulators(even_accs, odd_accs):
        def do_chunk(chunk, now, finishing):
            near = near_of(chunk - 1)
            slot = 1 - now

            @pl.when(chunk >= 3)
            def _():
                put(chunk - 3).wait()

            done = 0
            for block in range(blocks):
                rows = pl.ds(block * WIDE, WIDE)
                pltpu.matmul_push_rhs(cos_ref[rows, :], block % 2, 0)
                pltpu.matmul_push_rhs(sin_ref[rows, :], block % 2, 1)
                for source in range(CHUNK):
                    if finishing and (block * CHUNK + source) * CHUNK >= done * blocks * CHUNK and done < CHUNK:
                        finish(even_accs[slot][done], odd_accs[slot][done], near, done, slot)
                        done += 1
                    real, imag = cross(chunk * (CHUNK // 8) + source // 8, source % 8, block)
                    load = block % 2 if source == 0 else None
                    pltpu.matmul_acc_lhs(even_accs[now][source], real, load_staged_rhs=load)
                    pltpu.matmul_acc_lhs(odd_accs[now][source], imag, load_staged_rhs=load)

            @pl.when(chunk >= 1)
            def _():
                put(chunk - 1).start()

        def step(pair, carry):
            do_chunk(2 * pair, 0, True)
            do_chunk(2 * pair + 1, 1, True)
            return carry

        zero = jnp.zeros((half, WIDE), BF16)
        for unit, (table, accs) in enumerate(((cos_ref, even_accs), (sin_ref, odd_accs))):
            pltpu.matmul_push_rhs(table[0:WIDE, :], 0, unit)
            for source in range(CHUNK):
                pltpu.matmul_acc_lhs(accs[1][source], zero, load_staged_rhs=0 if source == 0 else None)
        lax.fori_loop(0, steps // 2, step, 0)
        last = steps - 1
        put(last - 2).wait()
        near = near_of(last)
        for source in range(CHUNK):
            finish(even_accs[1][source], odd_accs[1][source], near, source, last % 2)
        put(last).start()
        put(last - 1).wait()
        put(last).wait()

    pl.run_scoped(
        with_accumulators,
        [[pltpu.ACC(0)((half, LAGS // 2), F32) for _ in range(CHUNK)] for _ in range(2)],
        [[pltpu.ACC(1)((half, LAGS // 2), F32) for _ in range(CHUNK)] for _ in range(2)],
    )


def correlated(src, rcv, flags, mask, cos_table, sin_table):
    half = rcv.shape[1]
    args = (src.reshape(WIN, half // 8, 8, NS), rcv, flags, mask, cos_table, sin_table)
    return pl.pallas_call(
        correlate_kernel,
        out_shape=jax.ShapeDtypeStruct((half, half, LAGS), F32),
        in_specs=[VMEM] * 6,
        out_specs=pl.BlockSpec(memory_space=pl.ANY),
        scratch_shapes=[
            pltpu.VMEM((half, 128), F32),
            pltpu.VMEM((2, CHUNK, half, LAGS), F32),
            pltpu.SemaphoreType.DMA((2,)),
        ],
        compiler_params=pltpu.CompilerParams(vmem_limit_bytes=8 * 2**20),
    )(*args)

MESH = pl.DeviceIdType.MESH


def gather_kernel(mine_ref, first_ref, turn_ref, lag_first_ref, lag_turn_ref,
                  out_ref, table_ref, cos_ref, sin_ref, send_sems, recv_sems):
    s, r = lax.axis_index("src"), lax.axis_index("rcv")
    z, high = lax.div(s, 2), lax.rem(s, 2)
    low, y, core = lax.div(r, 8), lax.rem(lax.div(r, 2), 4), lax.rem(r, 2)

    def around(step):
        return (s, 8 * low + 2 * lax.rem(y + 4 + step, 4) + core)

    def along(step):
        return (2 * lax.rem(z + 8 + step, 8) + high, r)

    sibling = (s, 8 * low + 2 * y + 1 - core)
    beside = (s, 8 * (1 - low) + 2 * y + core)
    across = (2 * z + 1 - high, r)
    mirror = (r, s)

    def src_slot(step, other):
        column = 1 - low if other else low
        return core * 8 + column * 4 + lax.rem(y + 4 + step, 4)

    def rcv_slot(step, other):
        column = 1 - high if other else high
        return 16 + column * 8 + lax.rem(z + 8 + step, 8)

    peers = [sibling, beside, across, around(1), around(-1), along(1), along(-1)]
    barrier = pltpu.get_barrier_semaphore()
    for peer in peers:
        pl.semaphore_signal(barrier, inc=1, device_id=peer, device_id_type=MESH)

    @pl.when(s != r)
    def _():
        pl.semaphore_signal(barrier, inc=1, device_id=mirror, device_id_type=MESH)

    def copy(slot, device, source=None, sem=0):
        return pltpu.make_async_remote_copy(
            src_ref=out_ref.at[slot] if source is None else source,
            dst_ref=out_ref.at[slot], send_sem=send_sems.at[sem],
            recv_sem=recv_sems.at[slot], device_id=device, device_id_type=MESH)

    def arrive(slot):
        block = out_ref.at[slot]
        pltpu.make_async_copy(block, block, recv_sems.at[slot]).wait()

    own = src_slot(0, False)
    local = pltpu.make_async_copy(mine_ref, out_ref.at[own], recv_sems.at[own])
    local.start()
    width = 256
    blocks = iter(range(NF // width))

    def fill(count):
        for _ in range(count):
            block = next(blocks, None)
            if block is not None:
                fill_forward(first_ref, turn_ref, table_ref, block, width)

    pl.semaphore_wait(barrier, len(peers) + jnp.where(s == r, 0, 1))
    mirrored = copy(16 + lax.rem(r, 2) * 8 + lax.div(r, 2), mirror, mine_ref, 1)

    @pl.when(s != r)
    def _():
        mirrored.start()

    @pl.when(s == r)
    def _():
        slot = rcv_slot(0, False)
        pltpu.make_async_copy(mine_ref, out_ref.at[slot], recv_sems.at[slot]).start()

    for device in (beside, around(1), around(-1), sibling):
        copy(own, device, mine_ref).start()
    fill(1)
    arrive(rcv_slot(0, False))
    for device in (across, along(1), along(-1)):
        copy(rcv_slot(0, False), device).start()
    arrive(src_slot(0, True))
    for device in (around(1), around(-1), sibling):
        copy(src_slot(0, True), device).start()
    arrive(rcv_slot(0, True))
    for device in (along(1), along(-1)):
        copy(rcv_slot(0, True), device).start()
    fill(1)

    def pass_along(distance, last):
        for other in (False, True):
            for way in (1, -1):
                if last and (way == -1) != other:
                    continue
                slot = rcv_slot(-way * distance, other)
                arrive(slot)
                if distance < 3 or (distance == 3 and (way == -1) == other):
                    copy(slot, along(way)).start()

    for other in (False, True):
        for way in (1, -1):
            slot = src_slot(-way, other)
            arrive(slot)
            if (way == -1) == other:
                copy(slot, around(way)).start()
            copy(slot, sibling).start()
    pass_along(1, False)
    fill(1)
    for other in (False, True):
        slot = src_slot(2, other)
        arrive(slot)
        copy(slot, sibling).start()
    pass_along(2, False)
    fill(1)
    pass_along(3, False)
    fill(2)
    fill_lags(lag_first_ref, lag_turn_ref, cos_ref, sin_ref)
    for index in range(8):
        arrive((1 - core) * 8 + index)
    pass_along(4, True)
    local.wait()
    block = out_ref.at[pl.ds(0, 30)]
    pltpu.make_async_copy(block, block, send_sems.at[0]).wait()

    @pl.when(s != r)
    def _():
        mirrored.wait_send()


def gathered(mine, first, turn, lag_first, lag_turn):
    return pl.pallas_call(
        gather_kernel,
        out_shape=[
            jax.ShapeDtypeStruct((32,) + mine.shape, mine.dtype),
            jax.ShapeDtypeStruct((NS // 2, NS), BF16),
            jax.ShapeDtypeStruct((NF, LAGS // 2), BF16),
            jax.ShapeDtypeStruct((NF, LAGS // 2), BF16),
        ],
        in_specs=[VMEM] * 5,
        out_specs=[VMEM] * 4,
        scratch_shapes=[pltpu.SemaphoreType.DMA((2,)), pltpu.SemaphoreType.DMA((32,))],
        compiler_params=pltpu.CompilerParams(
            collective_id=0, has_side_effects=True, vmem_limit_bytes=16 * 2**20),
    )(mine, first, turn, lag_first, lag_turn)


def shards(traces, window_valid, pair_mask):
    marked = jnp.where(window_valid[:, :, None] != 0, traces, jnp.asarray(INVALID, traces.dtype))
    windows, channels, samples = traces.shape
    mine = marked.reshape(windows, channels, 2, samples // 2).transpose(2, 0, 1, 3)
    mine = mine.reshape(2 * windows * channels, samples // 2)
    first, turn, phase, lag_first, lag_turn = seeds()
    pieces, table, cos_table, sin_table = gathered(mine, first, turn, lag_first, lag_turn)
    src, rcv, flags = whitened(pieces, table, phase)
    return correlated(src, rcv, flags, pair_mask, cos_table, sin_table)


def solution(mesh):
    in_specs = (P(None, ("src", "rcv"), None), P(None, ("src", "rcv")), P("src", "rcv"))
    mapped = jax.shard_map(
        shards, mesh=mesh, in_specs=in_specs, out_specs=P("src", "rcv", None), check_vma=False)

    def run(traces, window_valid, pair_mask):
        with jax.sharding.use_abstract_mesh(mesh.abstract_mesh):
            return mapped(traces, window_valid, pair_mask)

    return run
```

time: 83.6 us -> 60.3 us (0.72)
  the two profiles are of different devices: /device:TPU:41 before, /device:TPU:24 now
where the time goes in v2:
time: 60.3 us; the launch traced here: 59.9 us
  Pallas kernels  54.1 us (90%)
  local copies, waits for them, and re-layouts  4.22 us (7%)
  other arithmetic  1.58 us (3%)
    pallas_call x1, Pallas kernels, gathered(): pl.pallas_call(gather_kernel, out_shape=[jax.ShapeDtypeStruct((32,) + min...  33.8 us
    pallas_call x1, Pallas kernels, correlated(): pl.pallas_call(correlate_kernel, out_shape=jax.ShapeDtypeStruct((half, ha...  10.6 us
    pallas_call x1, Pallas kernels, whitened(): pl.pallas_call(functools.partial(whiten_kernel, count), out_shape=[jax.Sh...  9.64 us
    unnamed x12, local copies, waits for them, and re-layouts  4.18 us

profile of v2, /device:TPU:24, one launch (start us, length us, event | category | flops | bytes accessed | tf_op | source)
XLA Modules:
  0.0 59.9 jit_solution(12801517837096807105)
XLA Ops:
  0.0 0.0 copy-start.3
  0.0 0.7 %broadcast_compare_fusion = pred[2,4]{1,0:T(4,128)(4,1)S(1)} fusion(s32[2,4]{1,0:T(2,128)} %param.9), kind=kLoop, calls=%fused_computation.2 | loop fusion | flops 8 | bytes 40 | tf_op jit(solution)/shard_map/ne | solution.py:454
  0.7 0.9 %broadcast_select_fusion = bf16[2,4,3072]{2,1,0:T(4,128)(2,1)S(1)} fusion(bf16[2,4,3072]{2,1,0:T(4,128)(2,1)} %param.8, pred[2,4]{1,0:T(4,128)(4,1)S(1)} %broadcast_compare_fusion), kind=kLoop, calls=%fused_computation.1 | loop fusion | flops 24576 | bytes 98312 | tf_op jit(solution)/shard_map/jit(_where)/select_n | solution.py:454
  1.6 0.0 copy-start
  1.6 0.9 %copy-done = f32[2,16,1536]{2,1,0:T(8,128)S(1)} copy-done((f32[2,16,1536]{2,1,0:T(8,128)S(1)}, f32[2,16,1536]{2,1,0:T(8,128)}, u32[]{:S(2)}) %copy-start) | copy-done | bytes 196632
  2.6 0.0 copy-start.2
  2.6 0.9 %copy-done.2 = f32[2,8,1536]{2,1,0:T(8,128)S(1)} copy-done((f32[2,8,1536]{2,1,0:T(8,128)S(1)}, f32[2,8,1536]{2,1,0:T(8,128)}, u32[]{:S(2)}) %copy-start.2) | copy-done | bytes 98328
  3.5 0.0 copy-start.4
  3.5 0.8 %copy-done.4 = f32[2,16,256]{2,1,0:T(8,128)S(1)} copy-done((f32[2,16,256]{2,1,0:T(8,128)S(1)}, f32[2,16,256]{2,1,0:T(8,128)}, u32[]{:S(2)}) %copy-start.4) | copy-done | bytes 32792
  4.2 0.0 copy-start.5
  4.2 0.7 %copy-done.5 = f32[2,8,256]{2,1,0:T(8,128)S(1)} copy-done((f32[2,8,256]{2,1,0:T(8,128)S(1)}, f32[2,8,256]{2,1,0:T(8,128)}, u32[]{:S(2)}) %copy-start.5) | copy-done | bytes 16408
  4.9 33.8 %shard_map.82 = (bf16[32,16,1536]{2,1,0:T(8,128)(2,1)S(1)}, bf16[1536,3072]{1,0:T(8,128)(2,1)S(1)}, bf16[1536,256]{1,0:T(8,128)(2,1)S(1)}, bf16[1536,256]{1,0:T(8,128)(2,1)S(1)}) custom-call(bf16[16,1536]{1,0:T(8,128)(2,1)S(1)} %reshape.12.mine_ref, f32[2,16,1536]{2,1,0:T(8,128)S(1)} %copy-done, f32[2,8,1536]{2,1,0:T(8,128)S(1)} %copy-done.2, ...), custom_call_target="tpu_custom_call" | custom-call | tf_op jit(solution)/shard_map/pallas_call | solution.py:437
  38.7 0.0 copy-start.1
  38.7 0.9 %copy-done.1 = f32[2,8,1536]{2,1,0:T(8,128)S(1)} copy-done((f32[2,8,1536]{2,1,0:T(8,128)S(1)}, f32[2,8,1536]{2,1,0:T(8,128)}, u32[]{:S(2)}) %copy-start.1) | copy-done | bytes 98328
  39.6 9.6 %shard_map.83 = (f32[2,64,3072]{2,1,0:T(8,128)S(1)}, bf16[2,64,3072]{2,1,0:T(8,128)(2,1)S(1)}, f32[128,128]{1,0:T(8,128)S(1)}) custom-call(bf16[32,16,1536]{2,1,0:T(8,128)(2,1)S(1)} %get-tuple-element.12.pieces_ref, bf16[1536,3072]{1,0:T(8,128)(2,1)S(1)} %get-tuple-element.13.table, f32[2,8,1536]{2,1,0:T(8,128)S(1)} %copy-done.1), custom_call_target="tpu_custom_call" | custom-call | tf_op jit(solution)/shard_map/pallas_call | solution.py:153
  49.3 0.0 copy-done.3
  49.3 10.6 %shard_map.84 = f32[64,64,512]{2,1,0:T(8,128)} custom-call(f32[2,8,8,3072]{3,2,1,0:T(8,128)S(1)} %bitcast.8, bf16[2,64,3072]{2,1,0:T(8,128)(2,1)S(1)} %get-tuple-element.15.rcv_ref, f32[128,128]{1,0:T(8,128)S(1)} %get-tuple-element.16.flags_ref, s32[64,64]{1,0:T(8,128)S(1)} %copy-done.3, bf16[1536,256]{1,0:T(8,128)(2,1)S(1)} %get-tuple-element.17.cos_ref, ...), custom_call_target="tpu_custom_call" | custom-call | tf_op jit(solution)/shard_map/pallas_call | solution.py:298
  (2 shorter events, 0.0 us)
Async XLA Ops:
  0.0 49.3 %copy-start.3 = (s32[64,64]{1,0:T(8,128)S(1)}, s32[64,64]{1,0:T(8,128)}, u32[]{:S(2)}) copy-start(s32[64,64]{1,0:T(8,128)} %mask_ref.1) | copy-start | bytes 49156
  1.6 0.9 %copy-start = (f32[2,16,1536]{2,1,0:T(8,128)S(1)}, f32[2,16,1536]{2,1,0:T(8,128)}, u32[]{:S(2)}) copy-start(f32[2,16,1536]{2,1,0:T(8,128)} %constant.14.clone.first_ref) | copy-start | bytes 589828
  2.6 0.9 %copy-start.2 = (f32[2,8,1536]{2,1,0:T(8,128)S(1)}, f32[2,8,1536]{2,1,0:T(8,128)}, u32[]{:S(2)}) copy-start(f32[2,8,1536]{2,1,0:T(8,128)} %constant.15.clone.turn_ref) | copy-start | bytes 294916
  3.5 0.8 %copy-start.4 = (f32[2,16,256]{2,1,0:T(8,128)S(1)}, f32[2,16,256]{2,1,0:T(8,128)}, u32[]{:S(2)}) copy-start(f32[2,16,256]{2,1,0:T(8,128)} %constant.16.clone.lag_first_ref) | copy-start | bytes 98308
  4.2 0.7 %copy-start.5 = (f32[2,8,256]{2,1,0:T(8,128)S(1)}, f32[2,8,256]{2,1,0:T(8,128)}, u32[]{:S(2)}) copy-start(f32[2,8,256]{2,1,0:T(8,128)} %constant.17.clone.lag_turn_ref) | copy-start | bytes 49156
  38.7 0.9 %copy-start.1 = (f32[2,8,1536]{2,1,0:T(8,128)S(1)}, f32[2,8,1536]{2,1,0:T(8,128)}, u32[]{:S(2)}) copy-start(f32[2,8,1536]{2,1,0:T(8,128)} %constant.18.clone.phase_ref) | copy-start | bytes 294916

commit v3 on v2

v3 whole, which is shorter than its diff:
```python
import functools
import math

import jax
import jax.numpy as jnp
import numpy as np
from jax import lax
from jax.experimental import pallas as pl
from jax.experimental.pallas import tpu as pltpu
from jax.sharding import PartitionSpec as P

NS = 3072
NF = 1536
LAGS = 512
HALF = 32
WIN = 2
EPSILON = 1e-06
STEP = 2.0 * math.pi / NS
INVALID = 100.0
F32 = jnp.float32
BF16 = jnp.bfloat16
VMEM = pl.BlockSpec(memory_space=pltpu.VMEM)


def cos_sin(angles):
    return np.stack([np.cos(angles), np.sin(angles)]).astype(np.float32)


def seeds():
    freqs = np.arange(1, NF + 1, dtype=np.float64) * STEP
    halves = np.arange(LAGS // 2, dtype=np.float64) + 0.5
    rows = np.zeros(32)
    rows[:16], rows[16:24], rows[24:] = np.arange(16), 16, 0.5
    lag_rows = np.full(24, 16 * STEP)
    lag_rows[:16] = freqs[:16]
    return cos_sin(rows[:, None] * freqs[None, :]), cos_sin(lag_rows[:, None] * halves[None, :])


def rotate(cosine, sine, turn_cos, turn_sin):
    return cosine * turn_cos - sine * turn_sin, sine * turn_cos + cosine * turn_sin


def fill_forward(seed, table, block, width):
    lanes = pl.ds(block * width, width)
    imag_lanes = pl.ds(NF + block * width, width)
    turn_cos, turn_sin = seed[0, 16:17, lanes], seed[1, 16:17, lanes]

    def rows(index, held):
        cosine, sine = held
        at = pl.ds(pl.multiple_of(index * 16, 16), 16)
        table[at, lanes] = cosine.astype(BF16)
        table[at, imag_lanes] = (-sine).astype(BF16)
        return rotate(cosine, sine, turn_cos, turn_sin)

    lax.fori_loop(0, NS // 32, rows, (seed[0, 0:16, lanes], seed[1, 0:16, lanes]))


def fill_lags(seed, cos_table, sin_table):
    turn_cos, turn_sin = seed[0, 16:17, :], seed[1, 16:17, :]

    def rows(index, held):
        cosine, sine = held
        at = pl.ds(pl.multiple_of(index * 16, 16), 16)
        cos_table[at, :] = cosine.astype(BF16)
        sin_table[at, :] = sine.astype(BF16)
        return rotate(cosine, sine, turn_cos, turn_sin)

    lax.fori_loop(0, NF // 16, rows, (seed[0, 0:16, :], seed[1, 0:16, :]))


def channel_group(slot):
    if slot < 16:
        core, low, y = slot // 8, slot // 4 % 2, slot % 4
        return 8 * low + 2 * y + core
    return slot % 8 * 2 + (slot - 16) // 8


def unpack(first_slot, count, pieces, flags_ref, ordered, left):
    for piece in range(count // 4):
        rows = pieces[first_slot + piece].astype(F32)
        first = 4 * channel_group(first_slot + piece)
        for part in range(4):
            ordered[part, first : first + 4, :] = rows[4 * part : 4 * part + 4]
    lane = lax.broadcasted_iota(jnp.int32, (count, 128), 1)
    flags = jnp.zeros((count, 128), F32)
    for window in range(WIN):
        valid = ordered[window, :, 0:1] < 0.5 * INVALID
        flags = jnp.where((lane == window) & valid, 1.0, flags)
        for part in (window, WIN + window):
            left[part * count : (part + 1) * count, :] = jnp.where(valid, ordered[part], 0.0).astype(BF16)
    flags_ref[...] = flags


def transform(block, left, table, spectrum, high, low):
    total = left.shape[0] // 2
    width = 256
    even = lax.broadcasted_iota(jnp.int32, (1, width), 1) % 2 == 0
    at = block * width
    square = None
    for base in (0, NF):
        lanes = slice(base + at, base + at + width)
        both = jnp.dot(left[...], table[:, lanes], preferred_element_type=F32)
        later = both[total:]
        value = both[:total] + jnp.where(even, -later, later)
        spectrum[:, lanes] = value
        square = value * value if square is None else square + value * value
    amplitude = jnp.sqrt(square)
    rounded = amplitude.astype(BF16)
    lanes = slice(128 + at, 128 + at + width)
    high[:, lanes] = rounded
    low[:, lanes] = (amplitude - rounded.astype(F32)).astype(BF16)


def pad(high, low):
    total = high.shape[0]
    for ref in (high, low):
        ref[:, 0:128] = jnp.zeros((total, 128), BF16)
        ref[:, 128 + NF : 256 + NF] = jnp.zeros((total, 128), BF16)


def band_table(width):
    offset = lax.broadcasted_iota(jnp.int32, (2 * width, width), 0) - lax.broadcasted_iota(
        jnp.int32, (2 * width, width), 1
    )
    return jnp.where((offset >= 128 - HALF) & (offset <= 128 + HALF), 1.0, 0.0).astype(BF16)


def smooth(block, spectrum, high, low, seed, src_ref, rcv_ref):
    width = 256
    band = band_table(width)
    at = block * width
    around = slice(at, at + 2 * width)
    running = jnp.dot(high[:, around], band, preferred_element_type=F32)
    running += jnp.dot(low[:, around], band, preferred_element_type=F32)
    factor = 1.0 / (running * (1.0 / (2 * HALF + 1)) + EPSILON)
    real_lanes = slice(at, at + width)
    imag_lanes = slice(NF + at, NF + at + width)
    real = (spectrum[:, real_lanes] * factor).astype(BF16)
    imag = (spectrum[:, imag_lanes] * factor).astype(BF16)
    half = real.shape[0] // WIN
    for window in range(WIN):
        rows = slice(window * half, window * half + half)
        if src_ref is not None:
            turn_cos, turn_sin = seed[0, 24:25, real_lanes], seed[1, 24:25, real_lanes]
            src_real, src_imag = real[rows].astype(F32), imag[rows].astype(F32)
            src_ref[window, :, real_lanes] = src_real * turn_cos + src_imag * turn_sin
            src_ref[window, :, imag_lanes] = src_imag * turn_cos - src_real * turn_sin
        else:
            rcv_ref[window, :, real_lanes] = real[rows]
            rcv_ref[window, :, imag_lanes] = imag[rows]


CHUNK = 8
WIDE = 256


def correlate_kernel(src_ref, rcv_ref, weights, cos_ref, sin_ref, out_ref, staged, out_sems):
    half = rcv_ref.shape[1]
    steps = half // CHUNK
    groups = half // 16
    blocks = NF // WIDE

    back = 127 - lax.broadcasted_iota(jnp.int32, (half, 128), 1)

    def finish(even_acc, odd_acc, near, source, slot):
        even, odd = pltpu.matmul_pop(even_acc), pltpu.matmul_pop(odd_acc)
        weight = jnp.broadcast_to(near[:, source : source + 1], (half, 128))
        width = LAGS // 2
        for block in range(width // 128):
            lanes = slice(block * 128, block * 128 + 128)
            e, o = even[:, lanes], odd[:, lanes]
            staged[slot, source, :, width + block * 128 : width + block * 128 + 128] = (e - o) * weight
            flipped = jnp.take_along_axis((e + o) * weight, back, axis=1)
            staged[slot, source, :, width - block * 128 - 128 : width - block * 128] = flipped

    def cross(eight, inside, block):
        real_rows, imag_rows = [], []
        halves = []
        for part in range(WIDE // 128):
            first = block * WIDE + part * 128
            lanes = (slice(first, first + 128), slice(NF + first, NF + first + 128))
            sent = [
                [
                    jnp.broadcast_to(src_ref[w, eight, inside : inside + 1, at], (16, 128)).astype(BF16)
                    for at in lanes
                ]
                for w in range(WIN)
            ]
            halves.append((lanes, sent))
        for g in range(groups):
            reals, imags = [], []
            for lanes, sent in halves:
                real = imag = None
                for w in range(WIN):
                    ar, ai = sent[w]
                    br, bi = (rcv_ref[w, 16 * g : 16 * g + 16, at] for at in lanes)
                    more_real = ar * br + ai * bi
                    more_imag = ai * br - ar * bi
                    real = more_real if real is None else real + more_real
                    imag = more_imag if imag is None else imag + more_imag
                reals.append(real)
                imags.append(imag)
            real_rows.append(jnp.concatenate(reals, axis=1))
            imag_rows.append(jnp.concatenate(imags, axis=1))
        return jnp.concatenate(real_rows, axis=0), jnp.concatenate(imag_rows, axis=0)

    def near_of(chunk):
        return pltpu.roll(weights[...], lax.rem(256 - chunk * CHUNK, 128), 1)

    def put(chunk):
        slot = chunk % 2 if isinstance(chunk, int) else lax.rem(chunk, 2)
        at = pl.ds(pl.multiple_of(chunk * CHUNK, CHUNK), CHUNK)
        return pltpu.make_async_copy(staged.at[slot], out_ref.at[at], out_sems.at[slot])

    def with_accumulators(even_accs, odd_accs):
        def do_chunk(chunk, now, finishing):
            near = near_of(chunk - 1)
            slot = 1 - now

            @pl.when(chunk >= 3)
            def _():
                put(chunk - 3).wait()

            done = 0
            for block in range(blocks):
                rows = pl.ds(block * WIDE, WIDE)
                pltpu.matmul_push_rhs(cos_ref[rows, :], block % 2, 0)
                pltpu.matmul_push_rhs(sin_ref[rows, :], block % 2, 1)
                for source in range(CHUNK):
                    if finishing and (block * CHUNK + source) * CHUNK >= done * blocks * CHUNK and done < CHUNK:
                        finish(even_accs[slot][done], odd_accs[slot][done], near, done, slot)
                        done += 1
                    real, imag = cross(chunk * (CHUNK // 8) + source // 8, source % 8, block)
                    load = block % 2 if source == 0 else None
                    pltpu.matmul_acc_lhs(even_accs[now][source], real, load_staged_rhs=load)
                    pltpu.matmul_acc_lhs(odd_accs[now][source], imag, load_staged_rhs=load)

            @pl.when(chunk >= 1)
            def _():
                put(chunk - 1).start()

        def step(pair, carry):
            do_chunk(2 * pair, 0, True)
            do_chunk(2 * pair + 1, 1, True)
            return carry

        zero = jnp.zeros((half, WIDE), BF16)
        for unit, (table, accs) in enumerate(((cos_ref, even_accs), (sin_ref, odd_accs))):
            pltpu.matmul_push_rhs(table[0:WIDE, :], 0, unit)
            for source in range(CHUNK):
                pltpu.matmul_acc_lhs(accs[1][source], zero, load_staged_rhs=0 if source == 0 else None)
        lax.fori_loop(0, steps // 2, step, 0)
        last = steps - 1
        put(last - 2).wait()
        near = near_of(last)
        for source in range(CHUNK):
            finish(even_accs[1][source], odd_accs[1][source], near, source, last % 2)
        put(last).start()
        put(last - 1).wait()
        put(last).wait()

    pl.run_scoped(
        with_accumulators,
        [[pltpu.ACC(0)((half, LAGS // 2), F32) for _ in range(CHUNK)] for _ in range(2)],
        [[pltpu.ACC(1)((half, LAGS // 2), F32) for _ in range(CHUNK)] for _ in range(2)],
    )


def correlated(src, rcv, weights, cos_table, sin_table):
    half = rcv.shape[1]
    args = (src.reshape(WIN, half // 8, 8, NS), rcv, weights, cos_table, sin_table)
    return pl.pallas_call(
        correlate_kernel,
        out_shape=jax.ShapeDtypeStruct((half, half, LAGS), F32),
        in_specs=[VMEM] * 5,
        out_specs=pl.BlockSpec(memory_space=pl.ANY),
        scratch_shapes=[
            pltpu.VMEM((2, CHUNK, half, LAGS), F32),
            pltpu.SemaphoreType.DMA((2,)),
        ],
        compiler_params=pltpu.CompilerParams(vmem_limit_bytes=8 * 2**20),
    )(*args)

MESH = pl.DeviceIdType.MESH


def spectra_kernel(traces_ref, valid_ref, seed_ref, lag_seed_ref, mask_ref,
                   src_ref, rcv_ref, weights_ref, cos_ref, sin_ref,
                   traces, valid, seed, lag_seed, mask, flags_ref, mine, pieces, table, ordered, left, spectrum, high, low_part,
                   local_sems, send_sems, recv_sems):
    s, r = lax.axis_index("src"), lax.axis_index("rcv")
    z, high_x = lax.div(s, 2), lax.rem(s, 2)
    low, y, core = lax.div(r, 8), lax.rem(lax.div(r, 2), 4), lax.rem(r, 2)

    def around(step):
        return (s, 8 * low + 2 * lax.rem(y + 4 + step, 4) + core)

    def along(step):
        return (2 * lax.rem(z + 8 + step, 8) + high_x, r)

    sibling = (s, 8 * low + 2 * y + 1 - core)
    beside = (s, 8 * (1 - low) + 2 * y + core)
    across = (2 * z + 1 - high_x, r)
    mirror = (r, s)

    def src_slot(step, other):
        column = 1 - low if other else low
        return core * 8 + column * 4 + lax.rem(y + 4 + step, 4)

    def rcv_slot(step, other):
        column = 1 - high_x if other else high_x
        return 16 + column * 8 + lax.rem(z + 8 + step, 8)

    loads = [
        pltpu.make_async_copy(source, target, local_sems.at[index])
        for index, (source, target) in enumerate(
            ((traces_ref, traces), (valid_ref, valid), (seed_ref, seed), (lag_seed_ref, lag_seed), (mask_ref, mask)))
    ]
    for load in loads:
        load.start()
    y_steps, z_steps = (1, -1, 2), (4, 3, -3, 2, -2, 1, -1)
    peers = [sibling, beside, across] + [around(k) for k in y_steps] + [along(k) for k in z_steps]
    barrier = pltpu.get_barrier_semaphore()
    for peer in peers:
        pl.semaphore_signal(barrier, inc=1, device_id=peer, device_id_type=MESH)

    @pl.when(s != r)
    def _():
        pl.semaphore_signal(barrier, inc=1, device_id=mirror, device_id_type=MESH)

    def copy(slot, device, source=None, sem=0):
        return pltpu.make_async_remote_copy(
            src_ref=pieces.at[slot] if source is None else source,
            dst_ref=pieces.at[slot], send_sem=send_sems.at[sem],
            recv_sem=recv_sems.at[slot], device_id=device, device_id_type=MESH)

    def arrive(slot):
        block = pieces.at[slot]
        pltpu.make_async_copy(block, block, recv_sems.at[slot]).wait()

    loads[0].wait()
    loads[1].wait()
    samples = NS // 2
    parts = []
    for window in range(WIN):
        rows = traces[window].astype(F32)
        keep = jnp.concatenate([valid[window : window + 1, c : c + 1] for c in range(rows.shape[0])], axis=0)
        parts.append(jnp.where(keep != 0, rows, INVALID))
    mine[...] = jnp.concatenate(
        [part[:, at : at + samples] for at in (0, samples) for part in parts], axis=0).astype(BF16)

    own = src_slot(0, False)
    local = pltpu.make_async_copy(mine, pieces.at[own], recv_sems.at[own])
    local.start()
    pl.semaphore_wait(barrier, len(peers) + jnp.where(s == r, 0, 1))
    mirrored = copy(16 + lax.rem(r, 2) * 8 + lax.div(r, 2), mirror, mine, 1)

    @pl.when(s != r)
    def _():
        mirrored.start()

    @pl.when(s == r)
    def _():
        slot = rcv_slot(0, False)
        pltpu.make_async_copy(mine, pieces.at[slot], recv_sems.at[slot]).start()

    for device in [beside] + [around(k) for k in y_steps] + [sibling]:
        copy(own, device, mine).start()
    loads[2].wait()
    loads[3].wait()
    width = 256
    blocks = NF // width
    filled = iter(range(blocks))

    def fill(count):
        for _ in range(count):
            fill_forward(seed, table, next(filled), width)

    def hand_over(steps):
        for step in steps:
            slot = rcv_slot(step, False)
            arrive(slot)
            copy(slot, across).start()

    fill(1)
    slot = rcv_slot(0, False)
    arrive(slot)
    for device in [along(k) for k in z_steps] + [across]:
        copy(slot, device).start()
    slot = src_slot(0, True)
    arrive(slot)
    for device in [around(k) for k in y_steps] + [sibling]:
        copy(slot, device).start()
    fill(2)
    for step in y_steps:
        slot = src_slot(step, False)
        arrive(slot)
        copy(slot, sibling).start()
    hand_over((1, -1))
    fill(1)
    for step in y_steps:
        slot = src_slot(step, True)
        arrive(slot)
        copy(slot, sibling).start()
    hand_over((2, -2))
    fill(2)
    fill_lags(lag_seed, cos_ref, sin_ref)
    pad(high, low_part)
    hand_over((3, -3))
    for index in range(8):
        arrive((1 - core) * 8 + index)
    local.wait()
    half = src_ref.shape[1]
    unpack(0, half, pieces, flags_ref.at[0:half], ordered, left)
    hand_over((4,))
    for block in range(blocks):
        transform(block, left, table, spectrum, high, low_part)
    for block in range(blocks):
        smooth(block, spectrum, high, low_part, seed, src_ref, None)
    for step in range(8):
        arrive(rcv_slot(step, True))
    unpack(16, half, pieces, flags_ref.at[half : 2 * half], ordered, left)
    loads[4].wait()
    flip = flags_ref[0:half, :].T
    counts = sum(flags_ref[half : 2 * half, w : w + 1] * flip[w : w + 1, :] for w in range(WIN))
    scale = mask[...].astype(F32).T * (1.0 / math.sqrt(NF)) / jnp.maximum(counts, 1.0)
    weights_ref[...] = jnp.concatenate([scale, jnp.zeros((half, 128 - half), F32)], axis=1)
    for block in range(blocks):
        transform(block, left, table, spectrum, high, low_part)
    for block in range(blocks):
        smooth(block, spectrum, high, low_part, seed, None, rcv_ref)
    block = pieces.at[pl.ds(0, 30)]
    pltpu.make_async_copy(block, block, send_sems.at[0]).wait()

    @pl.when(s != r)
    def _():
        mirrored.wait_send()


def spectra(half, traces, window_valid, pair_mask):
    seed, lag_seed = seeds()
    total = WIN * half
    far = pl.BlockSpec(memory_space=pltpu.HBM)
    rows = 2 * WIN * traces.shape[1]
    return pl.pallas_call(
        spectra_kernel,
        out_shape=[
            jax.ShapeDtypeStruct((WIN, half, NS), F32),
            jax.ShapeDtypeStruct((WIN, half, NS), BF16),
            jax.ShapeDtypeStruct((half, 128), F32),
            jax.ShapeDtypeStruct((NF, LAGS // 2), BF16),
            jax.ShapeDtypeStruct((NF, LAGS // 2), BF16),
        ],
        in_specs=[far] * 5,
        out_specs=[VMEM] * 5,
        scratch_shapes=[
            pltpu.VMEM(traces.shape, BF16),
            pltpu.VMEM(window_valid.shape, jnp.int32),
            pltpu.VMEM(seed.shape, F32),
            pltpu.VMEM(lag_seed.shape, F32),
            pltpu.VMEM(pair_mask.shape, jnp.int32),
            pltpu.VMEM((2 * half, 128), F32),
            pltpu.VMEM((rows, NS // 2), BF16),
            pltpu.VMEM((32, rows, NS // 2), BF16),
            pltpu.VMEM((NS // 2, NS), BF16),
            pltpu.VMEM((4, half, NS // 2), F32),
            pltpu.VMEM((2 * total, NS // 2), BF16),
            pltpu.VMEM((total, NS), F32),
            pltpu.VMEM((total, NF + 256), BF16),
            pltpu.VMEM((total, NF + 256), BF16),
            pltpu.SemaphoreType.DMA((5,)),
            pltpu.SemaphoreType.DMA((2,)),
            pltpu.SemaphoreType.DMA((32,)),
        ],
        compiler_params=pltpu.CompilerParams(
            collective_id=0, has_side_effects=True, vmem_limit_bytes=28 * 2**20),
    )(*(pltpu.with_memory_space_constraint(a, pltpu.HBM) for a in (traces, window_valid, jnp.asarray(seed), jnp.asarray(lag_seed), pair_mask)))


def shards(traces, window_valid, pair_mask):
    src, rcv, weights, cos_table, sin_table = spectra(pair_mask.shape[0], traces, window_valid, pair_mask)
    return correlated(src, rcv, weights, cos_table, sin_table)


def solution(mesh):
    in_specs = (P(None, ("src", "rcv"), None), P(None, ("src", "rcv")), P("src", "rcv"))
    mapped = jax.shard_map(
        shards, mesh=mesh, in_specs=in_specs, out_specs=P("src", "rcv", None), check_vma=False)

    def run(traces, window_valid, pair_mask):
        with jax.sharding.use_abstract_mesh(mesh.abstract_mesh):
            return mapped(traces, window_valid, pair_mask)

    return run
```

time: 60.3 us -> 49.4 us (0.82)
  the two profiles are of different devices: /device:TPU:24 before, /device:TPU:1 now
where the time goes in v3:
time: 49.4 us
  Pallas kernels  49.3 us (100%)
    pallas_call x1, Pallas kernels, spectra(): pl.pallas_call(spectra_kernel, out_shape=[jax.ShapeDtypeStruct((WIN, half...  38.7 us
    pallas_call x1, Pallas kernels, correlated(): pl.pallas_call(correlate_kernel, out_shape=jax.ShapeDtypeStruct((half, ha...  10.6 us

profile of v3, /device:TPU:1, one launch (start us, length us, event | category | flops | bytes accessed | tf_op | source)
XLA Modules:
  0.0 49.4 jit_solution(3087801856485632112)
XLA Ops:
  0.0 38.7 %shard_map.55 = (f32[2,64,3072]{2,1,0:T(8,128)S(1)}, bf16[2,64,3072]{2,1,0:T(8,128)(2,1)S(1)}, f32[64,128]{1,0:T(8,128)S(1)}, bf16[1536,256]{1,0:T(8,128)(2,1)S(1)}, bf16[1536,256]{1,0:T(8,128)(2,1)S(1)}) custom-call(bf16[2,4,3072]{2,1,0:T(4,128)(2,1)} %traces_ref.1, s32[2,4]{1,0:T(2,128)} %valid_ref.1, f32[2,32,1536]{2,1,0:T(8,128)} %constant.4.clone.seed_ref, ...), custom_call_target="tpu_custom_call" | custom-call | tf_op jit(solution)/shard_map/pallas_call | solution.py:445
  38.7 10.6 %shard_map.56 = f32[64,64,512]{2,1,0:T(8,128)} custom-call(f32[2,8,8,3072]{3,2,1,0:T(8,128)S(1)} %bitcast.1, bf16[2,64,3072]{2,1,0:T(8,128)(2,1)S(1)} %get-tuple-element.11.rcv_ref, f32[64,128]{1,0:T(8,128)S(1)} %get-tuple-element.12.weights, bf16[1536,256]{1,0:T(8,128)(2,1)S(1)} %get-tuple-element.13.cos_ref, bf16[1536,256]{1,0:T(8,128)(2,1)S(1)} %get-tuple-element.14.sin_ref), custom_call_target="tpu_custom_call" | custom-call | tf_op jit(solution)/shard_map/pallas_call | solution.py:272

commit v4 on v3

--- a/solution.py
+++ b/solution.py
@@ -69,46 +69,45 @@
 
 
 def channel_group(slot):
-    if slot < 16:
-        core, low, y = slot // 8, slot // 4 % 2, slot % 4
-        return 8 * low + 2 * y + core
-    return slot % 8 * 2 + (slot - 16) // 8
-
-
-def unpack(first_slot, count, pieces, flags_ref, ordered, left):
+    core, low, y = slot // 8, slot // 4 % 2, slot % 4
+    return 8 * low + 2 * y + core
+
+
+def unpack(count, slot_of, row_of, pieces, ordered, left):
     for piece in range(count // 4):
-        rows = pieces[first_slot + piece].astype(F32)
-        first = 4 * channel_group(first_slot + piece)
+        rows = pieces[slot_of(piece)].astype(F32)
+        first = row_of(piece)
         for part in range(4):
             ordered[part, first : first + 4, :] = rows[4 * part : 4 * part + 4]
     lane = lax.broadcasted_iota(jnp.int32, (count, 128), 1)
     flags = jnp.zeros((count, 128), F32)
     for window in range(WIN):
-        valid = ordered[window, :, 0:1] < 0.5 * INVALID
+        valid = ordered[window, 0:count, 0:1] < 0.5 * INVALID
         flags = jnp.where((lane == window) & valid, 1.0, flags)
         for part in (window, WIN + window):
-            left[part * count : (part + 1) * count, :] = jnp.where(valid, ordered[part], 0.0).astype(BF16)
-    flags_ref[...] = flags
-
-
-def transform(block, left, table, spectrum, high, low):
-    total = left.shape[0] // 2
+            rows = jnp.where(valid, ordered[part, 0:count, :], 0.0)
+            left[part * count : (part + 1) * count, :] = rows.astype(BF16)
+    return flags
+
+
+def transform(block, first, total, left, table, spectrum, high, low):
     width = 256
     even = lax.broadcasted_iota(jnp.int32, (1, width), 1) % 2 == 0
     at = block * width
     square = None
+    rows = slice(first, first + total)
     for base in (0, NF):
         lanes = slice(base + at, base + at + width)
-        both = jnp.dot(left[...], table[:, lanes], preferred_element_type=F32)
+        both = jnp.dot(left[0 : 2 * total, :], table[:, lanes], preferred_element_type=F32)
         later = both[total:]
         value = both[:total] + jnp.where(even, -later, later)
-        spectrum[:, lanes] = value
+        spectrum[rows, lanes] = value
         square = value * value if square is None else square + value * value
     amplitude = jnp.sqrt(square)
     rounded = amplitude.astype(BF16)
     lanes = slice(128 + at, 128 + at + width)
-    high[:, lanes] = rounded
-    low[:, lanes] = (amplitude - rounded.astype(F32)).astype(BF16)
+    high[rows, lanes] = rounded
+    low[rows, lanes] = (amplitude - rounded.astype(F32)).astype(BF16)
 
 
 def pad(high, low):
@@ -125,7 +124,7 @@
     return jnp.where((offset >= 128 - HALF) & (offset <= 128 + HALF), 1.0, 0.0).astype(BF16)
 
 
-def smooth(block, spectrum, high, low, seed, src_ref, rcv_ref):
+def whiten(block, spectrum, high, low):
     width = 256
     band = band_table(width)
     at = block * width
@@ -133,21 +132,39 @@
     running = jnp.dot(high[:, around], band, preferred_element_type=F32)
     running += jnp.dot(low[:, around], band, preferred_element_type=F32)
     factor = 1.0 / (running * (1.0 / (2 * HALF + 1)) + EPSILON)
-    real_lanes = slice(at, at + width)
-    imag_lanes = slice(NF + at, NF + at + width)
-    real = (spectrum[:, real_lanes] * factor).astype(BF16)
-    imag = (spectrum[:, imag_lanes] * factor).astype(BF16)
+    lanes = slice(at, at + width), slice(NF + at, NF + at + width)
+    return lanes, [spectrum[:, part] * factor for part in lanes]
+
+
+def put_sources(block, spectrum, high, low, seed, src_ref):
+    (real_lanes, imag_lanes), parts = whiten(block, spectrum, high, low)
+    real, imag = (part.astype(BF16).astype(F32) for part in parts)
+    turn_cos, turn_sin = seed[0, 24:25, real_lanes], seed[1, 24:25, real_lanes]
     half = real.shape[0] // WIN
     for window in range(WIN):
         rows = slice(window * half, window * half + half)
-        if src_ref is not None:
-            turn_cos, turn_sin = seed[0, 24:25, real_lanes], seed[1, 24:25, real_lanes]
-            src_real, src_imag = real[rows].astype(F32), imag[rows].astype(F32)
-            src_ref[window, :, real_lanes] = src_real * turn_cos + src_imag * turn_sin
-            src_ref[window, :, imag_lanes] = src_imag * turn_cos - src_real * turn_sin
-        else:
-            rcv_ref[window, :, real_lanes] = real[rows]
-            rcv_ref[window, :, imag_lanes] = imag[rows]
+        src_ref[window, :, real_lanes] = real[rows] * turn_cos + imag[rows] * turn_sin
+        src_ref[window, :, imag_lanes] = imag[rows] * turn_cos - real[rows] * turn_sin
+
+
+def interleave(own, other, high_x):
+    rows, width = own.shape
+    first = jnp.where(high_x == 0, own, other).reshape(rows // 8, 8, width)
+    second = jnp.where(high_x == 0, other, own).reshape(rows // 8, 8, width)
+    upper = lax.broadcasted_iota(jnp.int32, (1, 8, 1), 1) < 4
+    even = jnp.where(upper, first, pltpu.roll(second, 4, 1))
+    odd = jnp.where(upper, pltpu.roll(first, 4, 1), second)
+    return jnp.stack([even, odd], axis=1).reshape(2 * rows, width)
+
+
+def put_receivers(block, spectrum, high, low, high_x, rcv_ref):
+    lanes, parts = whiten(block, spectrum, high, low)
+    quarter = spectrum.shape[0] // 4
+    for at, part in zip(lanes, parts):
+        for window in range(WIN):
+            own = part[window * quarter : (window + 1) * quarter]
+            other = part[(2 + window) * quarter : (3 + window) * quarter]
+            rcv_ref[window, :, at] = interleave(own, other, high_x).astype(BF16)
 
 
 CHUNK = 8
@@ -318,7 +335,8 @@
     ]
     for load in loads:
         load.start()
-    y_steps, z_steps = (1, -1, 2), (4, 3, -3, 2, -2, 1, -1)
+    y_steps, z_steps = (1, -1, 2), (1, -1, 2, -2)
+    way = 1 - 2 * core
     peers = [sibling, beside, across] + [around(k) for k in y_steps] + [along(k) for k in z_steps]
     barrier = pltpu.get_barrier_semaphore()
     for peer in peers:
@@ -382,7 +400,9 @@
             arrive(slot)
             copy(slot, across).start()
 
-    fill(1)
+    fill(blocks)
+    fill_lags(lag_seed, cos_ref, sin_ref)
+    pad(high, low_part)
     slot = rcv_slot(0, False)
     arrive(slot)
     for device in [along(k) for k in z_steps] + [across]:
@@ -391,44 +411,53 @@
     arrive(slot)
     for device in [around(k) for k in y_steps] + [sibling]:
         copy(slot, device).start()
-    fill(2)
     for step in y_steps:
         slot = src_slot(step, False)
         arrive(slot)
         copy(slot, sibling).start()
     hand_over((1, -1))
-    fill(1)
+    for step, onward in ((-2 * way, (2 * way, way)), (2 * way, (-way,))):
+        slot = rcv_slot(step, False)
+        arrive(slot)
+        for further in onward:
+            copy(slot, along(further)).start()
+        copy(slot, across).start()
     for step in y_steps:
         slot = src_slot(step, True)
         arrive(slot)
         copy(slot, sibling).start()
-    hand_over((2, -2))
-    fill(2)
-    fill_lags(lag_seed, cos_ref, sin_ref)
-    pad(high, low_part)
-    hand_over((3, -3))
     for index in range(8):
         arrive((1 - core) * 8 + index)
     local.wait()
     half = src_ref.shape[1]
-    unpack(0, half, pieces, flags_ref.at[0:half], ordered, left)
-    hand_over((4,))
+    quarter = half // 2
+    flags_ref[0:half, :] = unpack(
+        half, lambda p: p, lambda p: 4 * channel_group(p), pieces, ordered, left)
     for block in range(blocks):
-        transform(block, left, table, spectrum, high, low_part)
+        transform(block, 0, 2 * half, left, table, spectrum, high, low_part)
+        if block == 1:
+            hand_over((3 * way, -3 * way))
+        if block == 3:
+            hand_over((4,))
     for block in range(blocks):
-        smooth(block, spectrum, high, low_part, seed, src_ref, None)
-    for step in range(8):
-        arrive(rcv_slot(step, True))
-    unpack(16, half, pieces, flags_ref.at[half : 2 * half], ordered, left)
+        put_sources(block, spectrum, high, low_part, seed, src_ref)
+    flags = []
+    for batch, column in enumerate((high_x, 1 - high_x)):
+        if batch == 1:
+            for step in range(8):
+                arrive(rcv_slot(step, True))
+        base = 16 + 8 * column
+        flags.append(unpack(quarter, lambda p: base + p, lambda p: 4 * p, pieces, ordered, left))
+        for block in range(blocks):
+            transform(block, batch * half, half, left, table, spectrum, high, low_part)
+    flags_ref[half : 2 * half, :] = interleave(flags[0], flags[1], high_x)
     loads[4].wait()
     flip = flags_ref[0:half, :].T
     counts = sum(flags_ref[half : 2 * half, w : w + 1] * flip[w : w + 1, :] for w in range(WIN))
     scale = mask[...].astype(F32).T * (1.0 / math.sqrt(NF)) / jnp.maximum(counts, 1.0)
     weights_ref[...] = jnp.concatenate([scale, jnp.zeros((half, 128 - half), F32)], axis=1)
     for block in range(blocks):
-        transform(block, left, table, spectrum, high, low_part)
-    for block in range(blocks):
-        smooth(block, spectrum, high, low_part, seed, None, rcv_ref)
+        put_receivers(block, spectrum, high, low_part, high_x, rcv_ref)
     block = pieces.at[pl.ds(0, 30)]
     pltpu.make_async_copy(block, block, send_sems.at[0]).wait()
 

time: 49.4 us -> 43.7 us (0.88); the launches traced: 49.4 us -> 42.9 us
  Pallas kernels: 49.3 us -> 42.9 us
    pallas_call x1, Pallas kernels: 38.7 us -> 32.3 us  [spectra(): pl.pallas_call(spectra_kernel, out_shape=[jax.ShapeDtypeStruct((WIN, half...]
where the time goes in v4:
time: 43.7 us; the launch traced here: 42.9 us
  Pallas kernels  42.9 us (98%)
    pallas_call x1, Pallas kernels, spectra(): pl.pallas_call(spectra_kernel, out_shape=[jax.ShapeDtypeStruct((WIN, half...  32.3 us
    pallas_call x1, Pallas kernels, correlated(): pl.pallas_call(correlate_kernel, out_shape=jax.ShapeDtypeStruct((half, ha...  10.6 us

profile of v4, /device:TPU:1, one launch (start us, length us, event | category | flops | bytes accessed | tf_op | source)
XLA Modules:
  0.0 42.9 jit_solution(12649846999765928263)
XLA Ops:
  0.0 32.3 %shard_map.55 = (f32[2,64,3072]{2,1,0:T(8,128)S(1)}, bf16[2,64,3072]{2,1,0:T(8,128)(2,1)S(1)}, f32[64,128]{1,0:T(8,128)S(1)}, bf16[1536,256]{1,0:T(8,128)(2,1)S(1)}, bf16[1536,256]{1,0:T(8,128)(2,1)S(1)}) custom-call(bf16[2,4,3072]{2,1,0:T(4,128)(2,1)} %traces_ref.1, s32[2,4]{1,0:T(2,128)} %valid_ref.1, f32[2,32,1536]{2,1,0:T(8,128)} %constant.4.clone.seed_ref, ...), custom_call_target="tpu_custom_call" | custom-call | tf_op jit(solution)/shard_map/pallas_call | solution.py:474
  32.3 10.6 %shard_map.56 = f32[64,64,512]{2,1,0:T(8,128)} custom-call(f32[2,8,8,3072]{3,2,1,0:T(8,128)S(1)} %bitcast.1, bf16[2,64,3072]{2,1,0:T(8,128)(2,1)S(1)} %get-tuple-element.11.rcv_ref, f32[64,128]{1,0:T(8,128)S(1)} %get-tuple-element.12.weights, bf16[1536,256]{1,0:T(8,128)(2,1)S(1)} %get-tuple-element.13.cos_ref, bf16[1536,256]{1,0:T(8,128)(2,1)S(1)} %get-tuple-element.14.sin_ref), custom_call_target="tpu_custom_call" | custom-call | tf_op jit(solution)/shard_map/pallas_call | solution.py:289

commit v5 on v4

--- a/solution.py
+++ b/solution.py
@@ -19,6 +19,7 @@
 INVALID = 100.0
 F32 = jnp.float32
 BF16 = jnp.bfloat16
+PARTS = 1
 VMEM = pl.BlockSpec(memory_space=pltpu.VMEM)
 
 
@@ -75,10 +76,13 @@
 
 def unpack(count, slot_of, row_of, pieces, ordered, left):
     for piece in range(count // 4):
-        rows = pieces[slot_of(piece)].astype(F32)
         first = row_of(piece)
-        for part in range(4):
-            ordered[part, first : first + 4, :] = rows[4 * part : 4 * part + 4]
+        width = NS // 2 // PARTS
+        for index in range(PARTS):
+            rows = pieces[slot_of(piece), index].astype(F32)
+            lanes = slice(index * width, index * width + width)
+            for part in range(4):
+                ordered[part, first : first + 4, lanes] = rows[4 * part : 4 * part + 4]
     lane = lax.broadcasted_iota(jnp.int32, (count, 128), 1)
     flags = jnp.zeros((count, 128), F32)
     for window in range(WIN):
@@ -171,7 +175,7 @@
 WIDE = 256
 
 
-def correlate_kernel(src_ref, rcv_ref, weights, cos_ref, sin_ref, out_ref, staged, out_sems):
+def correlate_kernel(src_ref, rcv_ref, weights, cos_ref, sin_ref, out_ref, staged, out_sems, last_sems):
     half = rcv_ref.shape[1]
     steps = half // CHUNK
     groups = half // 16
@@ -229,6 +233,10 @@
         at = pl.ds(pl.multiple_of(chunk * CHUNK, CHUNK), CHUNK)
         return pltpu.make_async_copy(staged.at[slot], out_ref.at[at], out_sems.at[slot])
 
+    def put_one(chunk, source):
+        return pltpu.make_async_copy(
+            staged.at[chunk % 2, source], out_ref.at[chunk * CHUNK + source], last_sems.at[source])
+
     def with_accumulators(even_accs, odd_accs):
         def do_chunk(chunk, now, finishing):
             near = near_of(chunk - 1)
@@ -261,20 +269,16 @@
             do_chunk(2 * pair + 1, 1, True)
             return carry
 
-        zero = jnp.zeros((half, WIDE), BF16)
-        for unit, (table, accs) in enumerate(((cos_ref, even_accs), (sin_ref, odd_accs))):
-            pltpu.matmul_push_rhs(table[0:WIDE, :], 0, unit)
-            for source in range(CHUNK):
-                pltpu.matmul_acc_lhs(accs[1][source], zero, load_staged_rhs=0 if source == 0 else None)
         lax.fori_loop(0, steps // 2, step, 0)
         last = steps - 1
         put(last - 2).wait()
         near = near_of(last)
         for source in range(CHUNK):
             finish(even_accs[1][source], odd_accs[1][source], near, source, last % 2)
-        put(last).start()
+            put_one(last, source).start()
         put(last - 1).wait()
-        put(last).wait()
+        for source in range(CHUNK):
+            put_one(last, source).wait()
 
     pl.run_scoped(
         with_accumulators,
@@ -294,6 +298,7 @@
         scratch_shapes=[
             pltpu.VMEM((2, CHUNK, half, LAGS), F32),
             pltpu.SemaphoreType.DMA((2,)),
+            pltpu.SemaphoreType.DMA((CHUNK,)),
         ],
         compiler_params=pltpu.CompilerParams(vmem_limit_bytes=8 * 2**20),
     )(*args)
@@ -335,9 +340,13 @@
     ]
     for load in loads:
         load.start()
-    y_steps, z_steps = (1, -1, 2), (1, -1, 2, -2)
+    y_steps, z_steps = (1, -1, 2), (2, -2, 1, -1)
     way = 1 - 2 * core
-    peers = [sibling, beside, across] + [around(k) for k in y_steps] + [along(k) for k in z_steps]
+    def diagonal(step):
+        return (2 * lax.rem(z + 8 + step, 8) + 1 - high_x, r)
+
+    peers = [diagonal(-way), diagonal(way), diagonal(-2 * way)]
+    peers += [sibling, beside, across] + [around(k) for k in y_steps] + [along(k) for k in z_steps]
     barrier = pltpu.get_barrier_semaphore()
     for peer in peers:
         pl.semaphore_signal(barrier, inc=1, device_id=peer, device_id_type=MESH)
@@ -346,15 +355,16 @@
     def _():
         pl.semaphore_signal(barrier, inc=1, device_id=mirror, device_id_type=MESH)
 
-    def copy(slot, device, source=None, sem=0):
+    def copy(slot, device, source=None, part=None, sem=0):
+        target = pieces.at[slot] if part is None else pieces.at[slot, part]
         return pltpu.make_async_remote_copy(
-            src_ref=pieces.at[slot] if source is None else source,
-            dst_ref=pieces.at[slot], send_sem=send_sems.at[sem],
-            recv_sem=recv_sems.at[slot], device_id=device, device_id_type=MESH)
-
-    def arrive(slot):
-        block = pieces.at[slot]
-        pltpu.make_async_copy(block, block, recv_sems.at[slot]).wait()
+            src_ref=target if source is None else source,
+            dst_ref=target, send_sem=send_sems.at[sem],
+            recv_sem=recv_sems.at[slot, part or 0], device_id=device, device_id_type=MESH)
+
+    def arrive(slot, part=None):
+        block = pieces.at[slot] if part is None else pieces.at[slot, part]
+        pltpu.make_async_copy(block, block, recv_sems.at[slot, part or 0]).wait()
 
     loads[0].wait()
     loads[1].wait()
@@ -364,26 +374,32 @@
         rows = traces[window].astype(F32)
         keep = jnp.concatenate([valid[window : window + 1, c : c + 1] for c in range(rows.shape[0])], axis=0)
         parts.append(jnp.where(keep != 0, rows, INVALID))
-    mine[...] = jnp.concatenate(
-        [part[:, at : at + samples] for at in (0, samples) for part in parts], axis=0).astype(BF16)
+    width = samples // PARTS
+    for index in range(PARTS):
+        starts = [first + index * width for first in (0, samples)]
+        mine[index] = jnp.concatenate(
+            [part[:, at : at + width] for at in starts for part in parts], axis=0).astype(BF16)
 
     own = src_slot(0, False)
-    local = pltpu.make_async_copy(mine, pieces.at[own], recv_sems.at[own])
+    local = pltpu.make_async_copy(mine, pieces.at[own], recv_sems.at[own, 0])
     local.start()
     pl.semaphore_wait(barrier, len(peers) + jnp.where(s == r, 0, 1))
-    mirrored = copy(16 + lax.rem(r, 2) * 8 + lax.div(r, 2), mirror, mine, 1)
+    mirrored = [
+        copy(16 + lax.rem(r, 2) * 8 + lax.div(r, 2), mirror, mine.at[part], part, 1 + part)
+        for part in range(PARTS)
+    ]
 
     @pl.when(s != r)
     def _():
-        mirrored.start()
+        for part in range(PARTS):
+            mirrored[part].start()
 
     @pl.when(s == r)
     def _():
         slot = rcv_slot(0, False)
-        pltpu.make_async_copy(mine, pieces.at[slot], recv_sems.at[slot]).start()
-
-    for device in [beside] + [around(k) for k in y_steps] + [sibling]:
-        copy(own, device, mine).start()
+        for part in range(PARTS):
+            pltpu.make_async_copy(mine.at[part], pieces.at[slot, part], recv_sems.at[slot, part]).start()
+
     loads[2].wait()
     loads[3].wait()
     width = 256
@@ -394,34 +410,38 @@
         for _ in range(count):
             fill_forward(seed, table, next(filled), width)
 
-    def hand_over(steps):
-        for step in steps:
-            slot = rcv_slot(step, False)
-            arrive(slot)
-            copy(slot, across).start()
-
-    fill(blocks)
+    fill(2)
+    for device in [beside] + [around(k) for k in y_steps] + [sibling]:
+        copy(own, device, mine).start()
+    fill(blocks - 2)
     fill_lags(lag_seed, cos_ref, sin_ref)
     pad(high, low_part)
     slot = rcv_slot(0, False)
-    arrive(slot)
-    for device in [along(k) for k in z_steps] + [across]:
-        copy(slot, device).start()
+    for part in range(PARTS):
+        arrive(slot, part)
+        for device in [along(k) for k in z_steps] + [across]:
+            copy(slot, device, None, part).start()
     slot = src_slot(0, True)
     arrive(slot)
     for device in [around(k) for k in y_steps] + [sibling]:
         copy(slot, device).start()
+    for part in range(PARTS):
+        for step, onward in ((-2 * way, (2 * way, way)), (2 * way, (-way,))):
+            slot = rcv_slot(step, False)
+            arrive(slot, part)
+            for further in onward:
+                copy(slot, along(further), None, part).start()
+                copy(slot, diagonal(further), None, part).start()
+            copy(slot, across, None, part).start()
+    slot = rcv_slot(0, True)
+    for part in range(PARTS):
+        arrive(slot, part)
+        for device in (along(1), along(-1)):
+            copy(slot, device, None, part).start()
     for step in y_steps:
         slot = src_slot(step, False)
         arrive(slot)
         copy(slot, sibling).start()
-    hand_over((1, -1))
-    for step, onward in ((-2 * way, (2 * way, way)), (2 * way, (-way,))):
-        slot = rcv_slot(step, False)
-        arrive(slot)
-        for further in onward:
-            copy(slot, along(further)).start()
-        copy(slot, across).start()
     for step in y_steps:
         slot = src_slot(step, True)
         arrive(slot)
@@ -435,17 +455,14 @@
         half, lambda p: p, lambda p: 4 * channel_group(p), pieces, ordered, left)
     for block in range(blocks):
         transform(block, 0, 2 * half, left, table, spectrum, high, low_part)
-        if block == 1:
-            hand_over((3 * way, -3 * way))
-        if block == 3:
-            hand_over((4,))
     for block in range(blocks):
         put_sources(block, spectrum, high, low_part, seed, src_ref)
     flags = []
     for batch, column in enumerate((high_x, 1 - high_x)):
-        if batch == 1:
-            for step in range(8):
-                arrive(rcv_slot(step, True))
+        for step in (1, 2, 3, 4, 5, 6, 7):
+            if batch == 1 or step not in (2, 6):
+                for part in range(PARTS):
+                    arrive(rcv_slot(step, batch == 1), part)
         base = 16 + 8 * column
         flags.append(unpack(quarter, lambda p: base + p, lambda p: 4 * p, pieces, ordered, left))
         for block in range(blocks):
@@ -463,7 +480,8 @@
 
     @pl.when(s != r)
     def _():
-        mirrored.wait_send()
+        for part in range(PARTS):
+            mirrored[part].wait_send()
 
 
 def spectra(half, traces, window_valid, pair_mask):
@@ -489,8 +507,8 @@
             pltpu.VMEM(lag_seed.shape, F32),
             pltpu.VMEM(pair_mask.shape, jnp.int32),
             pltpu.VMEM((2 * half, 128), F32),
-            pltpu.VMEM((rows, NS // 2), BF16),
-            pltpu.VMEM((32, rows, NS // 2), BF16),
+            pltpu.VMEM((PARTS, rows, NS // 2 // PARTS), BF16),
+            pltpu.VMEM((32, PARTS, rows, NS // 2 // PARTS), BF16),
             pltpu.VMEM((NS // 2, NS), BF16),
             pltpu.VMEM((4, half, NS // 2), F32),
             pltpu.VMEM((2 * total, NS // 2), BF16),
@@ -498,8 +516,8 @@
             pltpu.VMEM((total, NF + 256), BF16),
             pltpu.VMEM((total, NF + 256), BF16),
             pltpu.SemaphoreType.DMA((5,)),
-            pltpu.SemaphoreType.DMA((2,)),
-            pltpu.SemaphoreType.DMA((32,)),
+            pltpu.SemaphoreType.DMA((1 + PARTS,)),
+            pltpu.SemaphoreType.DMA((32, PARTS)),
         ],
         compiler_params=pltpu.CompilerParams(
             collective_id=0, has_side_effects=True, vmem_limit_bytes=28 * 2**20),

time: 43.7 us -> 42 us (0.961); the launches traced: 42.9 us -> 41.9 us
  Pallas kernels: 42.9 us -> 41.9 us
    pallas_call x1, Pallas kernels: 32.3 us -> 31.6 us  [spectra(): pl.pallas_call(spectra_kernel, out_shape=[jax.ShapeDtypeStruct((WIN, half...]
where the time goes in v5:
time: 42 us; the launch traced here: 41.9 us
  Pallas kernels  41.9 us (100%)
    pallas_call x1, Pallas kernels, spectra(): pl.pallas_call(spectra_kernel, out_shape=[jax.ShapeDtypeStruct((WIN, half...  31.6 us
    pallas_call x1, Pallas kernels, correlated(): pl.pallas_call(correlate_kernel, out_shape=jax.ShapeDtypeStruct((half, ha...  10.2 us

profile of v5, /device:TPU:1, one launch (start us, length us, event | category | flops | bytes accessed | tf_op | source)
XLA Modules:
  0.0 41.9 jit_solution(6595112081236946764)
XLA Ops:
  0.0 31.6 %shard_map.55 = (f32[2,64,3072]{2,1,0:T(8,128)S(1)}, bf16[2,64,3072]{2,1,0:T(8,128)(2,1)S(1)}, f32[64,128]{1,0:T(8,128)S(1)}, bf16[1536,256]{1,0:T(8,128)(2,1)S(1)}, bf16[1536,256]{1,0:T(8,128)(2,1)S(1)}) custom-call(bf16[2,4,3072]{2,1,0:T(4,128)(2,1)} %traces_ref.1, s32[2,4]{1,0:T(2,128)} %valid_ref.1, f32[2,32,1536]{2,1,0:T(8,128)} %constant.4.clone.seed_ref, ...), custom_call_target="tpu_custom_call" | custom-call | tf_op jit(solution)/shard_map/pallas_call | solution.py:492
  31.6 10.2 %shard_map.56 = f32[64,64,512]{2,1,0:T(8,128)} custom-call(f32[2,8,8,3072]{3,2,1,0:T(8,128)S(1)} %bitcast.1, bf16[2,64,3072]{2,1,0:T(8,128)(2,1)S(1)} %get-tuple-element.11.rcv_ref, f32[64,128]{1,0:T(8,128)S(1)} %get-tuple-element.12.weights, bf16[1536,256]{1,0:T(8,128)(2,1)S(1)} %get-tuple-element.13.cos_ref, bf16[1536,256]{1,0:T(8,128)(2,1)S(1)} %get-tuple-element.14.sin_ref), custom_call_target="tpu_custom_call" | custom-call | tf_op jit(solution)/shard_map/pallas_call | solution.py:293

commit v6 on v5

--- a/solution.py
+++ b/solution.py
@@ -94,24 +94,24 @@
     return flags
 
 
-def transform(block, first, total, left, table, spectrum, high, low):
+def transform(block, left, table, spectrum, high, low):
     width = 256
     even = lax.broadcasted_iota(jnp.int32, (1, width), 1) % 2 == 0
     at = block * width
     square = None
-    rows = slice(first, first + total)
+    total = spectrum.shape[0]
     for base in (0, NF):
         lanes = slice(base + at, base + at + width)
         both = jnp.dot(left[0 : 2 * total, :], table[:, lanes], preferred_element_type=F32)
         later = both[total:]
         value = both[:total] + jnp.where(even, -later, later)
-        spectrum[rows, lanes] = value
+        spectrum[:, lanes] = value
         square = value * value if square is None else square + value * value
     amplitude = jnp.sqrt(square)
     rounded = amplitude.astype(BF16)
     lanes = slice(128 + at, 128 + at + width)
-    high[rows, lanes] = rounded
-    low[rows, lanes] = (amplitude - rounded.astype(F32)).astype(BF16)
+    high[:, lanes] = rounded
+    low[:, lanes] = (amplitude - rounded.astype(F32)).astype(BF16)
 
 
 def pad(high, low):
@@ -151,24 +151,13 @@
         src_ref[window, :, imag_lanes] = imag[rows] * turn_cos - real[rows] * turn_sin
 
 
-def interleave(own, other, high_x):
-    rows, width = own.shape
-    first = jnp.where(high_x == 0, own, other).reshape(rows // 8, 8, width)
-    second = jnp.where(high_x == 0, other, own).reshape(rows // 8, 8, width)
-    upper = lax.broadcasted_iota(jnp.int32, (1, 8, 1), 1) < 4
-    even = jnp.where(upper, first, pltpu.roll(second, 4, 1))
-    odd = jnp.where(upper, pltpu.roll(first, 4, 1), second)
-    return jnp.stack([even, odd], axis=1).reshape(2 * rows, width)
-
-
-def put_receivers(block, spectrum, high, low, high_x, rcv_ref):
+def put_receivers(block, spectrum, high, low, first, rcv_ref):
     lanes, parts = whiten(block, spectrum, high, low)
-    quarter = spectrum.shape[0] // 4
+    count = spectrum.shape[0] // WIN
+    rows = pl.ds(pl.multiple_of(first, count), count)
     for at, part in zip(lanes, parts):
         for window in range(WIN):
-            own = part[window * quarter : (window + 1) * quarter]
-            other = part[(2 + window) * quarter : (3 + window) * quarter]
-            rcv_ref[window, :, at] = interleave(own, other, high_x).astype(BF16)
+            rcv_ref[window, rows, at] = part[window * count : (window + 1) * count].astype(BF16)
 
 
 CHUNK = 8
@@ -323,14 +312,18 @@
     sibling = (s, 8 * low + 2 * y + 1 - core)
     beside = (s, 8 * (1 - low) + 2 * y + core)
     across = (2 * z + 1 - high_x, r)
-    mirror = (r, s)
+    own_low = lax.rem(low + high_x + core, 2)
+    mirror_x = lax.rem(high_x + low + lax.div(z, 4), 2)
+    mirror = (2 * lax.rem(r, 8) + mirror_x, s)
+    mirrored_from = (r, 8 * own_low + z)
+    away = jnp.logical_or(mirror[0] != s, s != r)
 
     def src_slot(step, other):
         column = 1 - low if other else low
         return core * 8 + column * 4 + lax.rem(y + 4 + step, 4)
 
     def rcv_slot(step, other):
-        column = 1 - high_x if other else high_x
+        column = 1 - own_low if other else own_low
         return 16 + column * 8 + lax.rem(z + 8 + step, 8)
 
     loads = [
@@ -351,9 +344,9 @@
     for peer in peers:
         pl.semaphore_signal(barrier, inc=1, device_id=peer, device_id_type=MESH)
 
-    @pl.when(s != r)
+    @pl.when(away)
     def _():
-        pl.semaphore_signal(barrier, inc=1, device_id=mirror, device_id_type=MESH)
+        pl.semaphore_signal(barrier, inc=1, device_id=mirrored_from, device_id_type=MESH)
 
     def copy(slot, device, source=None, part=None, sem=0):
         target = pieces.at[slot] if part is None else pieces.at[slot, part]
@@ -383,18 +376,18 @@
     own = src_slot(0, False)
     local = pltpu.make_async_copy(mine, pieces.at[own], recv_sems.at[own, 0])
     local.start()
-    pl.semaphore_wait(barrier, len(peers) + jnp.where(s == r, 0, 1))
+    pl.semaphore_wait(barrier, len(peers) + jnp.where(away, 1, 0))
     mirrored = [
-        copy(16 + lax.rem(r, 2) * 8 + lax.div(r, 2), mirror, mine.at[part], part, 1 + part)
+        copy(16 + r, mirror, mine.at[part], part, 1 + part)
         for part in range(PARTS)
     ]
 
-    @pl.when(s != r)
+    @pl.when(away)
     def _():
         for part in range(PARTS):
             mirrored[part].start()
 
-    @pl.when(s == r)
+    @pl.when(jnp.logical_not(away))
     def _():
         slot = rcv_slot(0, False)
         for part in range(PARTS):
@@ -454,31 +447,31 @@
     flags_ref[0:half, :] = unpack(
         half, lambda p: p, lambda p: 4 * channel_group(p), pieces, ordered, left)
     for block in range(blocks):
-        transform(block, 0, 2 * half, left, table, spectrum, high, low_part)
+        transform(block, left, table, spectrum, high, low_part)
     for block in range(blocks):
         put_sources(block, spectrum, high, low_part, seed, src_ref)
-    flags = []
-    for batch, column in enumerate((high_x, 1 - high_x)):
-        for step in (1, 2, 3, 4, 5, 6, 7):
-            if batch == 1 or step not in (2, 6):
-                for part in range(PARTS):
-                    arrive(rcv_slot(step, batch == 1), part)
+    views = [ref.at[0:half] for ref in (spectrum, high, low_part)]
+    for batch, column in enumerate((own_low, 1 - own_low)):
+        for step in range(8):
+            if step not in ((0, 2, 6), (0,))[batch]:
+                arrive(rcv_slot(step, batch == 1), 0)
         base = 16 + 8 * column
-        flags.append(unpack(quarter, lambda p: base + p, lambda p: 4 * p, pieces, ordered, left))
+        first = quarter * column
+        flags_ref[pl.ds(pl.multiple_of(half + first, quarter), quarter), :] = unpack(
+            quarter, lambda p: base + p, lambda p: 4 * p, pieces, ordered, left)
         for block in range(blocks):
-            transform(block, batch * half, half, left, table, spectrum, high, low_part)
-    flags_ref[half : 2 * half, :] = interleave(flags[0], flags[1], high_x)
+            transform(block, left, table, *views)
+        for block in range(blocks):
+            put_receivers(block, *views, first, rcv_ref)
     loads[4].wait()
     flip = flags_ref[0:half, :].T
     counts = sum(flags_ref[half : 2 * half, w : w + 1] * flip[w : w + 1, :] for w in range(WIN))
     scale = mask[...].astype(F32).T * (1.0 / math.sqrt(NF)) / jnp.maximum(counts, 1.0)
     weights_ref[...] = jnp.concatenate([scale, jnp.zeros((half, 128 - half), F32)], axis=1)
-    for block in range(blocks):
-        put_receivers(block, spectrum, high, low_part, high_x, rcv_ref)
     block = pieces.at[pl.ds(0, 30)]
     pltpu.make_async_copy(block, block, send_sems.at[0]).wait()
 
-    @pl.when(s != r)
+    @pl.when(away)
     def _():
         for part in range(PARTS):
             mirrored[part].wait_send()

time: 42 us -> 41.5 us (0.988)
  Pallas kernels: 41.9 us -> 41.4 us
    pallas_call x1, Pallas kernels: 31.6 us -> 31.2 us  [spectra(): pl.pallas_call(spectra_kernel, out_shape=[jax.ShapeDtypeStruct((WIN, half...]
where the time goes in v6:
time: 41.5 us; the launch traced here: 41.4 us
  Pallas kernels  41.4 us (100%)
    pallas_call x1, Pallas kernels, spectra(): pl.pallas_call(spectra_kernel, out_shape=[jax.ShapeDtypeStruct((WIN, half...  31.2 us
    pallas_call x1, Pallas kernels, correlated(): pl.pallas_call(correlate_kernel, out_shape=jax.ShapeDtypeStruct((half, ha...  10.2 us

profile of v6, /device:TPU:1, one launch (start us, length us, event | category | flops | bytes accessed | tf_op | source)
XLA Modules:
  0.0 41.4 jit_solution(1081080185764791958)
XLA Ops:
  0.0 31.2 %shard_map.55 = (f32[2,64,3072]{2,1,0:T(8,128)S(1)}, bf16[2,64,3072]{2,1,0:T(8,128)(2,1)S(1)}, f32[64,128]{1,0:T(8,128)S(1)}, bf16[1536,256]{1,0:T(8,128)(2,1)S(1)}, bf16[1536,256]{1,0:T(8,128)(2,1)S(1)}) custom-call(bf16[2,4,3072]{2,1,0:T(4,128)(2,1)} %traces_ref.1, s32[2,4]{1,0:T(2,128)} %valid_ref.1, f32[2,32,1536]{2,1,0:T(8,128)} %constant.4.clone.seed_ref, ...), custom_call_target="tpu_custom_call" | custom-call | tf_op jit(solution)/shard_map/pallas_call | solution.py:485
  31.2 10.2 %shard_map.56 = f32[64,64,512]{2,1,0:T(8,128)} custom-call(f32[2,8,8,3072]{3,2,1,0:T(8,128)S(1)} %bitcast.1, bf16[2,64,3072]{2,1,0:T(8,128)(2,1)S(1)} %get-tuple-element.11.rcv_ref, f32[64,128]{1,0:T(8,128)S(1)} %get-tuple-element.12.weights, bf16[1536,256]{1,0:T(8,128)(2,1)S(1)} %get-tuple-element.13.cos_ref, bf16[1536,256]{1,0:T(8,128)(2,1)S(1)} %get-tuple-element.14.sin_ref), custom_call_target="tpu_custom_call" | custom-call | tf_op jit(solution)/shard_map/pallas_call | solution.py:282

commit v7 on v6

--- a/solution.py
+++ b/solution.py
@@ -16,10 +16,8 @@
 WIN = 2
 EPSILON = 1e-06
 STEP = 2.0 * math.pi / NS
-INVALID = 100.0
 F32 = jnp.float32
 BF16 = jnp.bfloat16
-PARTS = 1
 VMEM = pl.BlockSpec(memory_space=pltpu.VMEM)
 
 
@@ -74,22 +72,21 @@
     return 8 * low + 2 * y + core
 
 
-def unpack(count, slot_of, row_of, pieces, ordered, left):
+def unpack(count, slot_of, row_of, pieces, marks, ordered, left):
     for piece in range(count // 4):
-        first = row_of(piece)
-        width = NS // 2 // PARTS
-        for index in range(PARTS):
-            rows = pieces[slot_of(piece), index].astype(F32)
-            lanes = slice(index * width, index * width + width)
-            for part in range(4):
-                ordered[part, first : first + 4, lanes] = rows[4 * part : 4 * part + 4]
+        at = slice(row_of(piece), row_of(piece) + 4)
+        for window in range(WIN):
+            rows = pieces[slot_of(piece), window].astype(F32)
+            ordered[window, at, :] = rows[:, : NS // 2]
+            ordered[WIN + window, at, :] = rows[:, NS // 2 : NS]
+            marks[window, at, :] = rows[:, NS:]
     lane = lax.broadcasted_iota(jnp.int32, (count, 128), 1)
     flags = jnp.zeros((count, 128), F32)
     for window in range(WIN):
-        valid = ordered[window, 0:count, 0:1] < 0.5 * INVALID
-        flags = jnp.where((lane == window) & valid, 1.0, flags)
+        valid = marks[window, 0:count, :]
+        flags = jnp.where(lane == window, valid, flags)
         for part in (window, WIN + window):
-            rows = jnp.where(valid, ordered[part, 0:count, :], 0.0)
+            rows = jnp.where(valid[:, 0:1] != 0.0, ordered[part, 0:count, :], 0.0)
             left[part * count : (part + 1) * count, :] = rows.astype(BF16)
     return flags
 
@@ -140,6 +137,13 @@
     return lanes, [spectrum[:, part] * factor for part in lanes]
 
 
+def put_thirds(ref, window, rows, block, thirds):
+    width = 256
+    for index, third in enumerate(thirds):
+        at = index * NF + block * width
+        ref[window, rows, at : at + width] = third
+
+
 def put_sources(block, spectrum, high, low, seed, src_ref):
     (real_lanes, imag_lanes), parts = whiten(block, spectrum, high, low)
     real, imag = (part.astype(BF16).astype(F32) for part in parts)
@@ -147,17 +151,20 @@
     half = real.shape[0] // WIN
     for window in range(WIN):
         rows = slice(window * half, window * half + half)
-        src_ref[window, :, real_lanes] = real[rows] * turn_cos + imag[rows] * turn_sin
-        src_ref[window, :, imag_lanes] = imag[rows] * turn_cos - real[rows] * turn_sin
+        turned_real = real[rows] * turn_cos + imag[rows] * turn_sin
+        turned_imag = imag[rows] * turn_cos - real[rows] * turn_sin
+        put_thirds(src_ref, window, slice(None), block, (turned_real + turned_imag, turned_imag, turned_real))
 
 
 def put_receivers(block, spectrum, high, low, first, rcv_ref):
     lanes, parts = whiten(block, spectrum, high, low)
     count = spectrum.shape[0] // WIN
     rows = pl.ds(pl.multiple_of(first, count), count)
-    for at, part in zip(lanes, parts):
-        for window in range(WIN):
-            rcv_ref[window, rows, at] = part[window * count : (window + 1) * count].astype(BF16)
+    real, imag = (part.astype(BF16).astype(F32) for part in parts)
+    thirds = (real, real - imag, real + imag)
+    for window in range(WIN):
+        own = slice(window * count, (window + 1) * count)
+        put_thirds(rcv_ref, window, rows, block, [third[own].astype(BF16) for third in thirds])
 
 
 CHUNK = 8
@@ -188,7 +195,7 @@
         halves = []
         for part in range(WIDE // 128):
             first = block * WIDE + part * 128
-            lanes = (slice(first, first + 128), slice(NF + first, NF + first + 128))
+            lanes = [slice(base + first, base + first + 128) for base in (0, NF, 2 * NF)]
             sent = [
                 [
                     jnp.broadcast_to(src_ref[w, eight, inside : inside + 1, at], (16, 128)).astype(BF16)
@@ -200,14 +207,11 @@
         for g in range(groups):
             reals, imags = [], []
             for lanes, sent in halves:
-                real = imag = None
+                total = None
                 for w in range(WIN):
-                    ar, ai = sent[w]
-                    br, bi = (rcv_ref[w, 16 * g : 16 * g + 16, at] for at in lanes)
-                    more_real = ar * br + ai * bi
-                    more_imag = ai * br - ar * bi
-                    real = more_real if real is None else real + more_real
-                    imag = more_imag if imag is None else imag + more_imag
+                    terms = [a * rcv_ref[w, 16 * g : 16 * g + 16, at] for a, at in zip(sent[w], lanes)]
+                    total = terms if total is None else [x + y for x, y in zip(total, terms)]
+                real, imag = total[0] - total[1], total[0] - total[2]
                 reals.append(real)
                 imags.append(imag)
             real_rows.append(jnp.concatenate(reals, axis=1))
@@ -278,7 +282,7 @@
 
 def correlated(src, rcv, weights, cos_table, sin_table):
     half = rcv.shape[1]
-    args = (src.reshape(WIN, half // 8, 8, NS), rcv, weights, cos_table, sin_table)
+    args = (src.reshape(WIN, half // 8, 8, 3 * NF), rcv, weights, cos_table, sin_table)
     return pl.pallas_call(
         correlate_kernel,
         out_shape=jax.ShapeDtypeStruct((half, half, LAGS), F32),
@@ -297,7 +301,7 @@
 
 def spectra_kernel(traces_ref, valid_ref, seed_ref, lag_seed_ref, mask_ref,
                    src_ref, rcv_ref, weights_ref, cos_ref, sin_ref,
-                   traces, valid, seed, lag_seed, mask, flags_ref, mine, pieces, table, ordered, left, spectrum, high, low_part,
+                   valid, seed, lag_seed, mask, flags_ref, mine, pieces, marks, table, ordered, left, spectrum, high, low_part,
                    local_sems, send_sems, recv_sems):
     s, r = lax.axis_index("src"), lax.axis_index("rcv")
     z, high_x = lax.div(s, 2), lax.rem(s, 2)
@@ -329,7 +333,7 @@
     loads = [
         pltpu.make_async_copy(source, target, local_sems.at[index])
         for index, (source, target) in enumerate(
-            ((traces_ref, traces), (valid_ref, valid), (seed_ref, seed), (lag_seed_ref, lag_seed), (mask_ref, mask)))
+            ((traces_ref, mine.at[:, :, 0:NS]), (valid_ref, valid), (seed_ref, seed), (lag_seed_ref, lag_seed), (mask_ref, mask)))
     ]
     for load in loads:
         load.start()
@@ -348,51 +352,47 @@
     def _():
         pl.semaphore_signal(barrier, inc=1, device_id=mirrored_from, device_id_type=MESH)
 
-    def copy(slot, device, source=None, part=None, sem=0):
-        target = pieces.at[slot] if part is None else pieces.at[slot, part]
+    def copy(slot, device, source=None):
         return pltpu.make_async_remote_copy(
-            src_ref=target if source is None else source,
-            dst_ref=target, send_sem=send_sems.at[sem],
-            recv_sem=recv_sems.at[slot, part or 0], device_id=device, device_id_type=MESH)
-
-    def arrive(slot, part=None):
-        block = pieces.at[slot] if part is None else pieces.at[slot, part]
-        pltpu.make_async_copy(block, block, recv_sems.at[slot, part or 0]).wait()
-
+            src_ref=pieces.at[slot] if source is None else source,
+            dst_ref=pieces.at[slot], send_sem=send_sems.at[0],
+            recv_sem=recv_sems.at[slot], device_id=device, device_id_type=MESH)
+
+    def arrive(slot):
+        block = pieces.at[slot]
+        pltpu.make_async_copy(block, block, recv_sems.at[slot]).wait()
+
+    halves = (slice(0, NS), slice(NS, NS + 128))
+    home = rcv_slot(0, False)
+
+    def place(part, source):
+        away_copy = pltpu.make_async_remote_copy(
+            src_ref=source, dst_ref=pieces.at[16 + r, :, :, halves[part]], send_sem=send_sems.at[1 + part],
+            recv_sem=recv_sems.at[16 + r], device_id=mirror, device_id_type=MESH)
+
+        @pl.when(away)
+        def _():
+            away_copy.start()
+
+        @pl.when(jnp.logical_not(away))
+        def _():
+            target = pieces.at[home, :, :, halves[part]]
+            pltpu.make_async_copy(source, target, recv_sems.at[home]).start()
+
+        return away_copy
+
+    pl.semaphore_wait(barrier, len(peers) + jnp.where(away, 1, 0))
+    placed = [place(0, traces_ref)]
     loads[0].wait()
     loads[1].wait()
-    samples = NS // 2
-    parts = []
     for window in range(WIN):
-        rows = traces[window].astype(F32)
-        keep = jnp.concatenate([valid[window : window + 1, c : c + 1] for c in range(rows.shape[0])], axis=0)
-        parts.append(jnp.where(keep != 0, rows, INVALID))
-    width = samples // PARTS
-    for index in range(PARTS):
-        starts = [first + index * width for first in (0, samples)]
-        mine[index] = jnp.concatenate(
-            [part[:, at : at + width] for at in starts for part in parts], axis=0).astype(BF16)
-
+        count = valid.shape[1]
+        keep = jnp.concatenate([valid[window : window + 1, c : c + 1] for c in range(count)], axis=0)
+        mine[window, :, halves[1]] = jnp.broadcast_to(jnp.where(keep != 0, 1.0, 0.0), (count, 128)).astype(BF16)
+    placed.append(place(1, mine.at[:, :, halves[1]]))
     own = src_slot(0, False)
-    local = pltpu.make_async_copy(mine, pieces.at[own], recv_sems.at[own, 0])
+    local = pltpu.make_async_copy(mine, pieces.at[own], recv_sems.at[own])
     local.start()
-    pl.semaphore_wait(barrier, len(peers) + jnp.where(away, 1, 0))
-    mirrored = [
-        copy(16 + r, mirror, mine.at[part], part, 1 + part)
-        for part in range(PARTS)
-    ]
-
-    @pl.when(away)
-    def _():
-        for part in range(PARTS):
-            mirrored[part].start()
-
-    @pl.when(jnp.logical_not(away))
-    def _():
-        slot = rcv_slot(0, False)
-        for part in range(PARTS):
-            pltpu.make_async_copy(mine.at[part], pieces.at[slot, part], recv_sems.at[slot, part]).start()
-
     loads[2].wait()
     loads[3].wait()
     width = 256
@@ -410,27 +410,24 @@
     fill_lags(lag_seed, cos_ref, sin_ref)
     pad(high, low_part)
     slot = rcv_slot(0, False)
-    for part in range(PARTS):
-        arrive(slot, part)
-        for device in [along(k) for k in z_steps] + [across]:
-            copy(slot, device, None, part).start()
+    arrive(slot)
+    for device in [along(k) for k in z_steps] + [across]:
+        copy(slot, device).start()
     slot = src_slot(0, True)
     arrive(slot)
     for device in [around(k) for k in y_steps] + [sibling]:
         copy(slot, device).start()
-    for part in range(PARTS):
-        for step, onward in ((-2 * way, (2 * way, way)), (2 * way, (-way,))):
-            slot = rcv_slot(step, False)
-            arrive(slot, part)
-            for further in onward:
-                copy(slot, along(further), None, part).start()
-                copy(slot, diagonal(further), None, part).start()
-            copy(slot, across, None, part).start()
+    for step, onward in ((-2 * way, (2 * way, way)), (2 * way, (-way,))):
+        slot = rcv_slot(step, False)
+        arrive(slot)
+        for further in onward:
+            copy(slot, along(further)).start()
+            copy(slot, diagonal(further)).start()
+        copy(slot, across).start()
     slot = rcv_slot(0, True)
-    for part in range(PARTS):
-        arrive(slot, part)
-        for device in (along(1), along(-1)):
-            copy(slot, device, None, part).start()
+    arrive(slot)
+    for device in (along(1), along(-1)):
+        copy(slot, device).start()
     for step in y_steps:
         slot = src_slot(step, False)
         arrive(slot)
@@ -445,7 +442,7 @@
     half = src_ref.shape[1]
     quarter = half // 2
     flags_ref[0:half, :] = unpack(
-        half, lambda p: p, lambda p: 4 * channel_group(p), pieces, ordered, left)
+        half, lambda p: p, lambda p: 4 * channel_group(p), pieces, marks, ordered, left)
     for block in range(blocks):
         transform(block, left, table, spectrum, high, low_part)
     for block in range(blocks):
@@ -454,11 +451,11 @@
     for batch, column in enumerate((own_low, 1 - own_low)):
         for step in range(8):
             if step not in ((0, 2, 6), (0,))[batch]:
-                arrive(rcv_slot(step, batch == 1), 0)
+                arrive(rcv_slot(step, batch == 1))
         base = 16 + 8 * column
         first = quarter * column
         flags_ref[pl.ds(pl.multiple_of(half + first, quarter), quarter), :] = unpack(
-            quarter, lambda p: base + p, lambda p: 4 * p, pieces, ordered, left)
+            quarter, lambda p: base + p, lambda p: 4 * p, pieces, marks, ordered, left)
         for block in range(blocks):
             transform(block, left, table, *views)
         for block in range(blocks):
@@ -473,20 +470,20 @@
 
     @pl.when(away)
     def _():
-        for part in range(PARTS):
-            mirrored[part].wait_send()
+        for part in placed:
+            part.wait_send()
 
 
 def spectra(half, traces, window_valid, pair_mask):
     seed, lag_seed = seeds()
     total = WIN * half
     far = pl.BlockSpec(memory_space=pltpu.HBM)
-    rows = 2 * WIN * traces.shape[1]
+    slot = (WIN, traces.shape[1], NS + 128)
     return pl.pallas_call(
         spectra_kernel,
         out_shape=[
-            jax.ShapeDtypeStruct((WIN, half, NS), F32),
-            jax.ShapeDtypeStruct((WIN, half, NS), BF16),
+            jax.ShapeDtypeStruct((WIN, half, 3 * NF), F32),
+            jax.ShapeDtypeStruct((WIN, half, 3 * NF), BF16),
             jax.ShapeDtypeStruct((half, 128), F32),
             jax.ShapeDtypeStruct((NF, LAGS // 2), BF16),
             jax.ShapeDtypeStruct((NF, LAGS // 2), BF16),
@@ -494,14 +491,14 @@
         in_specs=[far] * 5,
         out_specs=[VMEM] * 5,
         scratch_shapes=[
-            pltpu.VMEM(traces.shape, BF16),
             pltpu.VMEM(window_valid.shape, jnp.int32),
             pltpu.VMEM(seed.shape, F32),
             pltpu.VMEM(lag_seed.shape, F32),
             pltpu.VMEM(pair_mask.shape, jnp.int32),
             pltpu.VMEM((2 * half, 128), F32),
-            pltpu.VMEM((PARTS, rows, NS // 2 // PARTS), BF16),
-            pltpu.VMEM((32, PARTS, rows, NS // 2 // PARTS), BF16),
+            pltpu.VMEM(slot, BF16),
+            pltpu.VMEM((32,) + slot, BF16),
+            pltpu.VMEM((WIN, half, 128), F32),
             pltpu.VMEM((NS // 2, NS), BF16),
             pltpu.VMEM((4, half, NS // 2), F32),
             pltpu.VMEM((2 * total, NS // 2), BF16),
@@ -509,8 +506,8 @@
             pltpu.VMEM((total, NF + 256), BF16),
             pltpu.VMEM((total, NF + 256), BF16),
             pltpu.SemaphoreType.DMA((5,)),
-            pltpu.SemaphoreType.DMA((1 + PARTS,)),
-            pltpu.SemaphoreType.DMA((32, PARTS)),
+            pltpu.SemaphoreType.DMA((3,)),
+            pltpu.SemaphoreType.DMA((32,)),
         ],
         compiler_params=pltpu.CompilerParams(
             collective_id=0, has_side_effects=True, vmem_limit_bytes=28 * 2**20),

time: 41.5 us -> 41 us (0.988)
    pallas_call x1, Pallas kernels: 10.2 us -> 9.34 us  [correlated(): pl.pallas_call(correlate_kernel, out_shape=jax.ShapeDtypeStruct((half, ha...]
    pallas_call x1, Pallas kernels: 31.2 us -> 31.6 us  [spectra(): pl.pallas_call(spectra_kernel, out_shape=[jax.ShapeDtypeStruct((WIN, half...]
where the time goes in v7:
time: 41 us
  Pallas kernels  41 us (100%)
    pallas_call x1, Pallas kernels, spectra(): pl.pallas_call(spectra_kernel, out_shape=[jax.ShapeDtypeStruct((WIN, half...  31.6 us
    pallas_call x1, Pallas kernels, correlated(): pl.pallas_call(correlate_kernel, out_shape=jax.ShapeDtypeStruct((half, ha...  9.34 us

profile of v7, /device:TPU:1, one launch (start us, length us, event | category | flops | bytes accessed | tf_op | source)
XLA Modules:
  0.0 41.0 jit_solution(7173313789258164763)
XLA Ops:
  0.0 31.6 %shard_map.55 = (f32[2,64,4608]{2,1,0:T(8,128)S(1)}, bf16[2,64,4608]{2,1,0:T(8,128)(2,1)S(1)}, f32[64,128]{1,0:T(8,128)S(1)}, bf16[1536,256]{1,0:T(8,128)(2,1)S(1)}, bf16[1536,256]{1,0:T(8,128)(2,1)S(1)}) custom-call(bf16[2,4,3072]{2,1,0:T(4,128)(2,1)} %traces_ref.1, s32[2,4]{1,0:T(2,128)} %valid_ref.1, f32[2,32,1536]{2,1,0:T(8,128)} %constant.4.clone.seed_ref, ...), custom_call_target="tpu_custom_call" | custom-call | tf_op jit(solution)/shard_map/pallas_call | solution.py:482
  31.6 9.3 %shard_map.56 = f32[64,64,512]{2,1,0:T(8,128)} custom-call(f32[2,8,8,4608]{3,2,1,0:T(8,128)S(1)} %bitcast.1, bf16[2,64,4608]{2,1,0:T(8,128)(2,1)S(1)} %get-tuple-element.11.rcv_ref, f32[64,128]{1,0:T(8,128)S(1)} %get-tuple-element.12.weights, bf16[1536,256]{1,0:T(8,128)(2,1)S(1)} %get-tuple-element.13.cos_ref, bf16[1536,256]{1,0:T(8,128)(2,1)S(1)} %get-tuple-element.14.sin_ref), custom_call_target="tpu_custom_call" | custom-call | tf_op jit(solution)/shard_map/pallas_call | solution.py:286

commit v8 on v6

--- a/solution.py
+++ b/solution.py
@@ -140,6 +140,13 @@
     return lanes, [spectrum[:, part] * factor for part in lanes]
 
 
+def put_thirds(ref, window, rows, block, thirds):
+    width = 256
+    for index, third in enumerate(thirds):
+        at = index * NF + block * width
+        ref[window, rows, at : at + width] = third
+
+
 def put_sources(block, spectrum, high, low, seed, src_ref):
     (real_lanes, imag_lanes), parts = whiten(block, spectrum, high, low)
     real, imag = (part.astype(BF16).astype(F32) for part in parts)
@@ -147,17 +154,20 @@
     half = real.shape[0] // WIN
     for window in range(WIN):
         rows = slice(window * half, window * half + half)
-        src_ref[window, :, real_lanes] = real[rows] * turn_cos + imag[rows] * turn_sin
-        src_ref[window, :, imag_lanes] = imag[rows] * turn_cos - real[rows] * turn_sin
+        turned_real = real[rows] * turn_cos + imag[rows] * turn_sin
+        turned_imag = imag[rows] * turn_cos - real[rows] * turn_sin
+        put_thirds(src_ref, window, slice(None), block, (turned_real + turned_imag, turned_imag, turned_real))
 
 
 def put_receivers(block, spectrum, high, low, first, rcv_ref):
     lanes, parts = whiten(block, spectrum, high, low)
     count = spectrum.shape[0] // WIN
     rows = pl.ds(pl.multiple_of(first, count), count)
-    for at, part in zip(lanes, parts):
-        for window in range(WIN):
-            rcv_ref[window, rows, at] = part[window * count : (window + 1) * count].astype(BF16)
+    real, imag = (part.astype(BF16) for part in parts)
+    thirds = (real, real - imag, real + imag)
+    for window in range(WIN):
+        own = slice(window * count, (window + 1) * count)
+        put_thirds(rcv_ref, window, rows, block, [third[own] for third in thirds])
 
 
 CHUNK = 8
@@ -188,7 +198,7 @@
         halves = []
         for part in range(WIDE // 128):
             first = block * WIDE + part * 128
-            lanes = (slice(first, first + 128), slice(NF + first, NF + first + 128))
+            lanes = [slice(base + first, base + first + 128) for base in (0, NF, 2 * NF)]
             sent = [
                 [
                     jnp.broadcast_to(src_ref[w, eight, inside : inside + 1, at], (16, 128)).astype(BF16)
@@ -200,14 +210,11 @@
         for g in range(groups):
             reals, imags = [], []
             for lanes, sent in halves:
-                real = imag = None
+                total = None
                 for w in range(WIN):
-                    ar, ai = sent[w]
-                    br, bi = (rcv_ref[w, 16 * g : 16 * g + 16, at] for at in lanes)
-                    more_real = ar * br + ai * bi
-                    more_imag = ai * br - ar * bi
-                    real = more_real if real is None else real + more_real
-                    imag = more_imag if imag is None else imag + more_imag
+                    terms = [a * rcv_ref[w, 16 * g : 16 * g + 16, at] for a, at in zip(sent[w], lanes)]
+                    total = terms if total is None else [x + y for x, y in zip(total, terms)]
+                real, imag = total[0] - total[1], total[0] - total[2]
                 reals.append(real)
                 imags.append(imag)
             real_rows.append(jnp.concatenate(reals, axis=1))
@@ -278,7 +285,7 @@
 
 def correlated(src, rcv, weights, cos_table, sin_table):
     half = rcv.shape[1]
-    args = (src.reshape(WIN, half // 8, 8, NS), rcv, weights, cos_table, sin_table)
+    args = (src.reshape(WIN, half // 8, 8, 3 * NF), rcv, weights, cos_table, sin_table)
     return pl.pallas_call(
         correlate_kernel,
         out_shape=jax.ShapeDtypeStruct((half, half, LAGS), F32),
@@ -450,6 +457,7 @@
         transform(block, left, table, spectrum, high, low_part)
     for block in range(blocks):
         put_sources(block, spectrum, high, low_part, seed, src_ref)
+    loads[4].wait()
     views = [ref.at[0:half] for ref in (spectrum, high, low_part)]
     for batch, column in enumerate((own_low, 1 - own_low)):
         for step in range(8):
@@ -459,15 +467,15 @@
         first = quarter * column
         flags_ref[pl.ds(pl.multiple_of(half + first, quarter), quarter), :] = unpack(
             quarter, lambda p: base + p, lambda p: 4 * p, pieces, ordered, left)
+        if batch == 1:
+            flip = flags_ref[0:half, :].T
+            counts = sum(flags_ref[half : 2 * half, w : w + 1] * flip[w : w + 1, :] for w in range(WIN))
+            scale = mask[...].astype(F32).T * (1.0 / math.sqrt(NF)) / jnp.maximum(counts, 1.0)
+            weights_ref[...] = jnp.concatenate([scale, jnp.zeros((half, 128 - half), F32)], axis=1)
         for block in range(blocks):
             transform(block, left, table, *views)
         for block in range(blocks):
             put_receivers(block, *views, first, rcv_ref)
-    loads[4].wait()
-    flip = flags_ref[0:half, :].T
-    counts = sum(flags_ref[half : 2 * half, w : w + 1] * flip[w : w + 1, :] for w in range(WIN))
-    scale = mask[...].astype(F32).T * (1.0 / math.sqrt(NF)) / jnp.maximum(counts, 1.0)
-    weights_ref[...] = jnp.concatenate([scale, jnp.zeros((half, 128 - half), F32)], axis=1)
     block = pieces.at[pl.ds(0, 30)]
     pltpu.make_async_copy(block, block, send_sems.at[0]).wait()
 
@@ -485,8 +493,8 @@
     return pl.pallas_call(
         spectra_kernel,
         out_shape=[
-            jax.ShapeDtypeStruct((WIN, half, NS), F32),
-            jax.ShapeDtypeStruct((WIN, half, NS), BF16),
+            jax.ShapeDtypeStruct((WIN, half, 3 * NF), F32),
+            jax.ShapeDtypeStruct((WIN, half, 3 * NF), BF16),
             jax.ShapeDtypeStruct((half, 128), F32),
             jax.ShapeDtypeStruct((NF, LAGS // 2), BF16),
             jax.ShapeDtypeStruct((NF, LAGS // 2), BF16),

time: 41.5 us -> 40.5 us (0.976)
  Pallas kernels: 41.4 us -> 40.4 us
    pallas_call x1, Pallas kernels: 10.2 us -> 9.33 us  [correlated(): pl.pallas_call(correlate_kernel, out_shape=jax.ShapeDtypeStruct((half, ha...]
where the time goes in v8:
time: 40.5 us; the launch traced here: 40.4 us
  Pallas kernels  40.4 us (100%)
    pallas_call x1, Pallas kernels, spectra(): pl.pallas_call(spectra_kernel, out_shape=[jax.ShapeDtypeStruct((WIN, half...  31.1 us
    pallas_call x1, Pallas kernels, correlated(): pl.pallas_call(correlate_kernel, out_shape=jax.ShapeDtypeStruct((half, ha...  9.33 us

profile of v8, /device:TPU:1, one launch (start us, length us, event | category | flops | bytes accessed | tf_op | source)
XLA Modules:
  0.0 40.4 jit_solution(15771255204234038482)
XLA Ops:
  0.0 31.1 %shard_map.55 = (f32[2,64,4608]{2,1,0:T(8,128)S(1)}, bf16[2,64,4608]{2,1,0:T(8,128)(2,1)S(1)}, f32[64,128]{1,0:T(8,128)S(1)}, bf16[1536,256]{1,0:T(8,128)(2,1)S(1)}, bf16[1536,256]{1,0:T(8,128)(2,1)S(1)}) custom-call(bf16[2,4,3072]{2,1,0:T(4,128)(2,1)} %traces_ref.1, s32[2,4]{1,0:T(2,128)} %valid_ref.1, f32[2,32,1536]{2,1,0:T(8,128)} %constant.4.clone.seed_ref, ...), custom_call_target="tpu_custom_call" | custom-call | tf_op jit(solution)/shard_map/pallas_call | solution.py:493
  31.1 9.3 %shard_map.56 = f32[64,64,512]{2,1,0:T(8,128)} custom-call(f32[2,8,8,4608]{3,2,1,0:T(8,128)S(1)} %bitcast.1, bf16[2,64,4608]{2,1,0:T(8,128)(2,1)S(1)} %get-tuple-element.11.rcv_ref, f32[64,128]{1,0:T(8,128)S(1)} %get-tuple-element.12.weights, bf16[1536,256]{1,0:T(8,128)(2,1)S(1)} %get-tuple-element.13.cos_ref, bf16[1536,256]{1,0:T(8,128)(2,1)S(1)} %get-tuple-element.14.sin_ref), custom_call_target="tpu_custom_call" | custom-call | tf_op jit(solution)/shard_map/pallas_call | solution.py:289

commit v9 on v8

--- a/solution.py
+++ b/solution.py
@@ -410,21 +410,29 @@
         for _ in range(count):
             fill_forward(seed, table, next(filled), width)
 
-    fill(2)
     for device in [beside] + [around(k) for k in y_steps] + [sibling]:
         copy(own, device, mine).start()
-    fill(blocks - 2)
+    fill(3)
+    slot = src_slot(0, True)
+    arrive(slot)
+    for device in [around(k) for k in y_steps] + [sibling]:
+        copy(slot, device).start()
+    fill(blocks - 3)
     fill_lags(lag_seed, cos_ref, sin_ref)
     pad(high, low_part)
+    for step in y_steps:
+        slot = src_slot(step, False)
+        arrive(slot)
+        copy(slot, sibling).start()
     slot = rcv_slot(0, False)
     for part in range(PARTS):
         arrive(slot, part)
         for device in [along(k) for k in z_steps] + [across]:
             copy(slot, device, None, part).start()
-    slot = src_slot(0, True)
-    arrive(slot)
-    for device in [around(k) for k in y_steps] + [sibling]:
-        copy(slot, device).start()
+    for step in y_steps:
+        slot = src_slot(step, True)
+        arrive(slot)
+        copy(slot, sibling).start()
     for part in range(PARTS):
         for step, onward in ((-2 * way, (2 * way, way)), (2 * way, (-way,))):
             slot = rcv_slot(step, False)
@@ -438,14 +446,6 @@
         arrive(slot, part)
         for device in (along(1), along(-1)):
             copy(slot, device, None, part).start()
-    for step in y_steps:
-        slot = src_slot(step, False)
-        arrive(slot)
-        copy(slot, sibling).start()
-    for step in y_steps:
-        slot = src_slot(step, True)
-        arrive(slot)
-        copy(slot, sibling).start()
     for index in range(8):
         arrive((1 - core) * 8 + index)
     local.wait()

time: 40.5 us -> 40.4 us (level)
  the two profiles are of different devices: /device:TPU:1 before, /device:TPU:32 now
where the time goes in v9:
time: 40.4 us; the launch traced here: 40.3 us
  Pallas kernels  40.3 us (100%)
    pallas_call x1, Pallas kernels, spectra(): pl.pallas_call(spectra_kernel, out_shape=[jax.ShapeDtypeStruct((WIN, half...  30.9 us
    pallas_call x1, Pallas kernels, correlated(): pl.pallas_call(correlate_kernel, out_shape=jax.ShapeDtypeStruct((half, ha...  9.33 us

profile of v9, /device:TPU:32, one launch (start us, length us, event | category | flops | bytes accessed | tf_op | source)
XLA Modules:
  0.0 40.3 jit_solution(1768602195260911800)
XLA Ops:
  0.0 30.9 %shard_map.55 = (f32[2,64,4608]{2,1,0:T(8,128)S(1)}, bf16[2,64,4608]{2,1,0:T(8,128)(2,1)S(1)}, f32[64,128]{1,0:T(8,128)S(1)}, bf16[1536,256]{1,0:T(8,128)(2,1)S(1)}, bf16[1536,256]{1,0:T(8,128)(2,1)S(1)}) custom-call(bf16[2,4,3072]{2,1,0:T(4,128)(2,1)} %traces_ref.1, s32[2,4]{1,0:T(2,128)} %valid_ref.1, f32[2,32,1536]{2,1,0:T(8,128)} %constant.4.clone.seed_ref, ...), custom_call_target="tpu_custom_call" | custom-call | tf_op jit(solution)/shard_map/pallas_call | solution.py:493
  30.9 9.3 %shard_map.56 = f32[64,64,512]{2,1,0:T(8,128)} custom-call(f32[2,8,8,4608]{3,2,1,0:T(8,128)S(1)} %bitcast.1, bf16[2,64,4608]{2,1,0:T(8,128)(2,1)S(1)} %get-tuple-element.11.rcv_ref, f32[64,128]{1,0:T(8,128)S(1)} %get-tuple-element.12.weights, bf16[1536,256]{1,0:T(8,128)(2,1)S(1)} %get-tuple-element.13.cos_ref, bf16[1536,256]{1,0:T(8,128)(2,1)S(1)} %get-tuple-element.14.sin_ref), custom_call_target="tpu_custom_call" | custom-call | tf_op jit(solution)/shard_map/pallas_call | solution.py:289
